TPU v7x, 512 devices: a whole 4x4x16 slice. The times are simulated.
512 devices in a mesh: gauss: 128 (over x, z, core), img: 4 (over y).
Axes of the slice: x: 4, y: 4, z: 16, core: 2. Of those that a mesh axis runs over, the one named last changes fastest.
Arguments:
- params: float32 [59, 524288], P(None, 'gauss'), as said below
- cameras: float32 [4, 16], P('img'), as said below
- send_rows: int32 [4, 65536], P('img', 'gauss'), may hold values from 0 to 4095
- tile_ids: int32 [4, 256], P('img', 'gauss'), may hold values from 0 to 255, as said below
- lists: int32 [4, 256, 256], P('img', 'gauss'), may hold values from 0 to 511, as said below
- counts: int32 [4, 256], P('img', 'gauss'), may hold values from 1 to 256, as said below
- targets: float32 [4, 256, 3, 256], P('img', 'gauss'), may hold values from -3 to 4
Outputs:
- grads: float32 [59, 524288], P(None, ('gauss', 'img'))
- rendered: float32 [4, 256, 3, 256], P('img', 'gauss')
Inputs may be any that keep to these rules, and one draw needn't show every extreme that they name: `params`: means at depth 3 to 5 in front of every view; log scales within -4.5 and -3.2, quaternion with w in [1, 2] and x, y, z in [-1, 1], opacity logits within -4 and -1, coefficients of order one. `cameras`: rotation by angles of at most 0.006 about each axis, translation entries within 0.02, focal lengths 255 to 257, centre at the middle of the image of 16 x 16 tiles, at pixel (128, 128). `tile_ids`: a permutation of the view's tiles; the 2 tiles of one owner form one of 128 groups of tiles that are the same in every view. `lists`: row s * 4 + k of a tile owner's received rows comes from Gaussian owner s; of every sender's 4 rows, each run of 2 belongs to one of the owner's tiles, a list names only rows of its own tile's runs, and its valid entries are distinct. `counts`: a tile has the same count in every view; in every view all tiles of one owner have the most, and another tile has 1.
All inputs are finite; a program needn't handle non-finite values.
Results may differ from a plain program's by a relative error of at most 0.0045.
Values sent between devices are 32-bit elements; how exact they have to be, the bound alone decides.
A program may use at most 64 MiB of HBM per device.

v0:
```python
import jax
import jax.numpy as jnp
from jax import lax
from jax.sharding import PartitionSpec as P

sh_zero = 0.28209479177387814
sh_one = 0.4886025119029199
sh_two = [
    1.0925484305920792,
    -1.0925484305920792,
    0.31539156525252005,
    -1.0925484305920792,
    0.5462742152960396,
]
sh_three = [
    -0.5900435899266435,
    2.890611442640554,
    -0.4570457994644658,
    0.3731763325901154,
    -0.4570457994644658,
    1.445305721320277,
    -0.5900435899266435,
]


def sum_terms(basis, coeffs):
    accum = basis[0][None, :] * coeffs[0]
    for k in range(1, 16):
        accum = accum + basis[k][None, :] * coeffs[k]
    return accum


def project(rows, camera):
    world = [rows[0], rows[1], rows[2]]
    rotation = [[camera[3 * i + j] for j in range(3)] for i in range(3)]
    shift = [camera[9], camera[10], camera[11]]
    focal_x, focal_y, centre_x, centre_y = (camera[12], camera[13], camera[14], camera[15])
    in_camera = [
        rotation[i][0] * world[0] + rotation[i][1] * world[1] + rotation[i][2] * world[2] + shift[i]
        for i in range(3)
    ]
    depth = in_camera[2]
    pos_u = focal_x * in_camera[0] / depth + centre_x
    pos_v = focal_y * in_camera[1] / depth + centre_y
    zero_row = jnp.zeros_like(depth)
    jacobian = [
        [focal_x / depth, zero_row, -focal_x * in_camera[0] / (depth * depth)],
        [zero_row, focal_y / depth, -focal_y * in_camera[1] / (depth * depth)],
    ]
    quat = rows[6:10]
    qnorm = jnp.sqrt(jnp.sum(quat * quat, axis=0))
    q_w, q_x, q_y, q_z = (quat[0] / qnorm, quat[1] / qnorm, quat[2] / qnorm, quat[3] / qnorm)
    rot_gauss = [
        [
            1.0 - 2.0 * (q_y * q_y + q_z * q_z),
            2.0 * (q_x * q_y - q_w * q_z),
            2.0 * (q_x * q_z + q_w * q_y),
        ],
        [
            2.0 * (q_x * q_y + q_w * q_z),
            1.0 - 2.0 * (q_x * q_x + q_z * q_z),
            2.0 * (q_y * q_z - q_w * q_x),
        ],
        [
            2.0 * (q_x * q_z - q_w * q_y),
            2.0 * (q_y * q_z + q_w * q_x),
            1.0 - 2.0 * (q_x * q_x + q_y * q_y),
        ],
    ]
    scales = jnp.exp(rows[3:6])
    screen_map = [
        [
            jacobian[a][0] * rotation[0][j]
            + jacobian[a][1] * rotation[1][j]
            + jacobian[a][2] * rotation[2][j]
            for j in range(3)
        ]
        for a in range(2)
    ]
    spread = [
        [
            (
                screen_map[a][0] * rot_gauss[0][k]
                + screen_map[a][1] * rot_gauss[1][k]
                + screen_map[a][2] * rot_gauss[2][k]
            )
            * scales[k]
            for k in range(3)
        ]
        for a in range(2)
    ]
    cov_xx = (
        spread[0][0] * spread[0][0]
        + spread[0][1] * spread[0][1]
        + spread[0][2] * spread[0][2]
        + 0.3
    )
    cov_xy = spread[0][0] * spread[1][0] + spread[0][1] * spread[1][1] + spread[0][2] * spread[1][2]
    cov_yy = (
        spread[1][0] * spread[1][0]
        + spread[1][1] * spread[1][1]
        + spread[1][2] * spread[1][2]
        + 0.3
    )
    determ = cov_xx * cov_yy - cov_xy * cov_xy
    opacity = jax.nn.sigmoid(rows[10])
    centre = [
        -(rotation[0][j] * shift[0] + rotation[1][j] * shift[1] + rotation[2][j] * shift[2])
        for j in range(3)
    ]
    view = [world[j] - centre[j] for j in range(3)]
    length = jnp.sqrt(view[0] * view[0] + view[1] * view[1] + view[2] * view[2])
    dir_x, dir_y, dir_z = (view[0] / length, view[1] / length, view[2] / length)
    sq_x, sq_y, sq_z = (dir_x * dir_x, dir_y * dir_y, dir_z * dir_z)
    basis = [
        sh_zero + zero_row,
        -sh_one * dir_y,
        sh_one * dir_z,
        -sh_one * dir_x,
        sh_two[0] * dir_x * dir_y,
        sh_two[1] * dir_y * dir_z,
        sh_two[2] * (2.0 * sq_z - sq_x - sq_y),
        sh_two[3] * dir_x * dir_z,
        sh_two[4] * (sq_x - sq_y),
        sh_three[0] * dir_y * (3.0 * sq_x - sq_y),
        sh_three[1] * dir_x * dir_y * dir_z,
        sh_three[2] * dir_y * (4.0 * sq_z - sq_x - sq_y),
        sh_three[3] * dir_z * (2.0 * sq_z - 3.0 * sq_x - 3.0 * sq_y),
        sh_three[4] * dir_x * (4.0 * sq_z - sq_x - sq_y),
        sh_three[5] * dir_z * (sq_x - sq_y),
        sh_three[6] * dir_x * (sq_x - 3.0 * sq_y),
    ]
    coeffs = rows[11:].reshape(16, 3, rows.shape[1])
    colour = 0.5 + sum_terms(basis, coeffs)
    return jnp.stack(
        [
            pos_u,
            pos_v,
            cov_yy / determ,
            -cov_xy / determ,
            cov_xx / determ,
            colour[0],
            colour[1],
            colour[2],
            opacity,
        ]
    )


def advance(carry, block_rows, start, pixel_x, pixel_y, count_now, strict_upper):
    log_trans, colour = carry
    width = block_rows.shape[1]
    off_x = block_rows[0][None, :] - pixel_x[:, None]
    off_y = block_rows[1][None, :] - pixel_y[:, None]
    quad = (
        block_rows[2] * off_x * off_x
        + 2.0 * block_rows[3] * off_x * off_y
        + block_rows[4] * off_y * off_y
    )
    live = (start + jnp.arange(width, dtype=jnp.int32) < count_now).astype(jnp.float32)
    alpha = live[None, :] * block_rows[8][None, :] * jnp.exp(-0.5 * quad)
    log_keep = jnp.log1p(-alpha)
    before = jnp.dot(log_keep, strict_upper, precision=lax.Precision.HIGHEST)
    weight = alpha * jnp.exp(log_trans[:, None] + before)
    colour = colour + jnp.dot(block_rows[5:8], weight.T, precision=lax.Precision.HIGHEST)
    return (log_trans + jnp.sum(log_keep, axis=1), colour)


def render_slots(slot_rows, tiles_dev, counts_dev):
    slot_count, feat_count, list_len = slot_rows.shape
    block_len = min(256, list_len)
    nblocks = list_len // block_len
    pixel = jnp.arange(256, dtype=jnp.int32)
    pixel_x = (tiles_dev[:, None] % 16 * 16 + pixel[None, :] % 16).astype(jnp.float32)
    pixel_y = (tiles_dev[:, None] // 16 * 16 + pixel[None, :] // 16).astype(jnp.float32)
    stacked = slot_rows.reshape(slot_count, feat_count, nblocks, block_len).transpose(2, 0, 1, 3)
    starts = jnp.arange(nblocks, dtype=jnp.int32) * block_len
    iota = jnp.arange(block_len, dtype=jnp.int32)
    strict_upper = (iota[:, None] < iota[None, :]).astype(jnp.float32)
    batched = jax.vmap(advance, in_axes=(0, 0, None, 0, 0, 0, None))

    def step(carry, inputs):
        block_rows, start = inputs
        updated = batched(carry, block_rows, start, pixel_x, pixel_y, counts_dev, strict_upper)
        return (updated, None)

    init = (jnp.zeros((slot_count, 256), jnp.float32), jnp.zeros((slot_count, 3, 256), jnp.float32))
    final, unused = lax.scan(step, init, (stacked, starts))
    return final[1]


def composite(features, lists_dev, counts_dev, tiles_dev, targets_dev):
    slot_rows = jnp.take(features, lists_dev, axis=1).transpose(1, 0, 2)
    colours, slot_back = jax.vjp(lambda rows: render_slots(rows, tiles_dev, counts_dev), slot_rows)
    grad_slots = slot_back(colours - targets_dev)[0]
    flat_grads = grad_slots.transpose(1, 0, 2).reshape(features.shape[0], -1)
    grad_feats = jnp.zeros_like(features).at[:, lists_dev.reshape(-1)].add(flat_grads)
    return (grad_feats, colours)


def local(params, cameras, send_rows, tile_ids, lists, counts, targets):
    camera = cameras[0]
    chosen = send_rows[0]
    outgoing = jnp.take(params, chosen, axis=1)
    received = lax.all_to_all(outgoing, "gauss", split_axis=1, concat_axis=1, tiled=True)
    features, pullback = jax.vjp(lambda rows: project(rows, camera), received)
    grad_feats, colours = composite(features, lists[0], counts[0], tile_ids[0], targets[0])
    grad_rows = lax.all_to_all(
        pullback(grad_feats)[0], "gauss", split_axis=1, concat_axis=1, tiled=True
    )
    local_sum = jnp.zeros_like(params).at[:, chosen].add(grad_rows)
    summed = lax.psum_scatter(local_sum, "img", scatter_dimension=1, tiled=True)
    return (summed, colours[None])


def solution(mesh):
    placed = (
        P(None, "gauss"),
        P("img", None),
        P("img", "gauss"),
        P("img", "gauss"),
        P("img", "gauss", None),
        P("img", "gauss"),
        P("img", "gauss", None, None),
    )
    return jax.shard_map(
        local,
        mesh=mesh,
        in_specs=placed,
        out_specs=(P(None, ("gauss", "img")), P("img", "gauss", None, None)),
        check_vma=False,
    )
```

profile of v0, /device:TPU:1, one launch (start us, length us, event | category | flops | bytes accessed | tf_op | source)
XLA Modules:
  0.0 267.8 jit_solution(18346889527606628839)
XLA Ops:
  8.4 1.3 reduce.25
  9.9 1.9 copy.478
  11.8 1.0 gather_fusion
  13.0 1.0 reshape.2684
  14.0 20.4 %all-to-all-start = ((f32[128,1,236]{2,1,0:T(1,128)}), f32[128,1,236]{2,1,0:T(1,128)S(1)}, u32[]{:S(2)}, u32[]{:S(2)}) async-start(f32[128,1,236]{2,1,0:T(1,128)} %reshape.2684), calls=%async_computation | async-start | bytes 262144 | tf_op jit(solution)/shard_map/all_to_all | solution.py:205
  54.4 0.9 reduce.26
  55.5 0.9 fusion.127
  57.8 2.2 fusion.128
  64.8 6.2 %multiply_add_fusion.3 = (f32[1,128,4]{1,2,0:T(4,128)}, f32[1,128,4]{1,2,0:T(4,128)}, f32[1,128,4]{1,2,0:T(4,128)}, f32[1,128,4]{1,2,0:T(4,128)S(1)}) fusion(f32[]{:T(128)S(6)} %broadcast_in_dim.211, f32[]{:T(128)} %bitcast.11, f32[]{:T(128)} %bitcast.12, f32[]{:T(128)} %bitcast.20, f32[]{:T(128)S(6)} %neg.445, f32[]{:T(128)} %bitcast.7, ...), kind=kLoop, calls=%fused_computation.214 | loop fusion | flops 10240 | bytes 14380 | tf_op jit(solution)/shard_map/jvp()/add | solution.py:73
  71.7 4.4 %multiply_add_fusion.1 = (f32[1,128,4]{1,2,0:T(4,128)}, f32[1,128,4]{1,2,0:T(4,128)}, f32[1,128,4]{1,2,0:T(4,128)}, f32[1,128,4]{1,2,0:T(4,128)S(1)}, f32[1,128,4]{1,2,0:T(4,128)S(1)}, /*index=5*/f32[1,128,4]{1,2,0:T(4,128)S(1)}) fusion(f32[]{:T(128)S(6)} %broadcast_in_dim.214, f32[]{:T(128)} %bitcast.12, f32[]{:T(128)} %bitcast.10, ...), kind=kLoop, calls=%fused_computation.212 | loop fusion | flops 8704 | bytes 20524 | tf_op jit(solution)/shard_map/jvp()/add | solution.py:73
  80.6 3.4 %fusion.129 = (f32[3,128,4]{0,2,1:T(4,128)S(1)}, f32[3,128,4]{0,2,1:T(4,128)S(1)}, f32[3,128,4]{0,2,1:T(4,128)S(1)}, f32[3,128,4]{0,2,1:T(4,128)S(1)}, f32[3,128...) fusion(f32[59,128,4]{0,2,1:T(4,128)S(1)} %bitcast.174), kind=kLoop, calls=%fused_computation.391 | loop fusion | flops 1536 | bytes 208896 | tf_op jit(solution)/shard_map/jvp()/slice | solution.py:29
  84.1 1.1 slice_reduce_fusion.2
  85.2 1.5 slice.329
  86.7 1.5 squeeze.175
  90.4 1.0 copy.538
  91.5 1.3 broadcast_multiply_fusion.3
  92.8 0.8 copy.489
  93.7 0.8 copy.488
  94.6 0.9 add.2220
  96.0 6.3 %multiply_add_fusion.4 = (f32[1,128,4]{1,2,0:T(4,128)}, f32[1,128,4]{1,2,0:T(4,128)}, f32[1,128,4]{1,2,0:T(4,128)}, f32[1,128,4]{1,2,0:T(4,128)}, f32[1,128,4]{1,2,0:T(4,128)S(1)}) fusion(f32[]{:T(128)S(6)} %broadcast_in_dim.210, f32[]{:T(128)} %bitcast.6, f32[]{:T(128)} %bitcast.8, f32[1,128,4]{1,2,0:T(4,128)S(1)} %get-tuple-element.203, f32[]{:T(128)} %bitcast.20, ...), kind=kLoop, calls=%fused_computation.215 | loop fusion | flops 11264 | bytes 18480 | tf_op jit(solution)/shard_map/jvp()/add | solution.py:73
  102.6 2.4 broadcast_divide_fusion.2
  105.1 0.9 copy.493
  105.9 0.9 copy.492
  106.8 0.9 copy.497
  107.6 7.0 %fusion.125 = (f32[1,512]{1,0:T(1,128)S(1)}, f32[1,512]{1,0:T(1,128)S(1)}, f32[1,512]{1,0:T(1,128)}, f32[1,512]{1,0:T(1,128)S(1)}, f32[1,512]{1,0:T(1,128)}, /*i...) fusion(f32[1,512]{1,0:T(1,128)} %slice.329, ...), kind=kLoop, calls=%fused_computation.387 | loop fusion | flops 58880 | bytes 90172 | tf_op jit(solution)/shard_map/jvp()/div | solution.py:141
  114.7 0.9 copy.495
  115.6 0.9 copy.496
  116.5 0.9 copy.494
  118.8 3.2 %add_add_fusion = f32[3,512]{0,1:T(8,128)} fusion(f32[3,512]{0,1:T(8,128)} %bitcast.202, f32[3,512]{0,1:T(8,128)} %bitcast.204, f32[3,512]{0,1:T(8,128)S(1)} %bitcast.178, f32[3,512]{0,1:T(8,128)S(1)} %bitcast.180, f32[3,512]{0,1:T(8,128)S(1)} %bitcast.182, f32[3,512]{0,1:T(8,128)S(1)} %bitcast.184, f32[3,512]{0,1:T(8,128)S(1)} %bitcast.186, ...), kind=kLoop, calls=%fused_computation.116 | loop fusion | flops 47616 | bytes 135168 | tf_op jit(solution)/shard_map/jvp()/add | solution.py:134
  122.0 1.9 stack.3
  124.0 1.6 gather_fusion.1
  125.7 1.1 copy.499
  126.9 0.8 convolution_exponential_fusion
  128.5 0.8 fusion.28
  129.3 2.1 copy.501
  132.1 2.6 fusion.23
  134.7 0.9 fusion.31
  135.9 0.9 copy.503
  136.7 2.7 %scatter_custom_fusion = f32[9,512]{0,1:T(8,128)S(1)} fusion(s32[512]{0:T(512)} %bitcast.241, f32[512,9]{1,0:T(8,128)} %copy.503, f32[]{:T(128)} %constant.171.clone.1), kind=kCustom, calls=%fused_computation.121 | custom fusion | flops 4608 | bytes 18944 | tf_op jit(solution)/shard_map/scatter-add | solution.py:197
  139.5 1.7 fusion.126
  141.5 1.7 multiply_reduce_fusion.10
  143.2 1.9 multiply_bitcast_fusion.14
  145.1 1.1 copy.528
  147.7 0.8 copy.515
  155.2 1.1 copy.539
  156.9 1.1 copy.541
  158.0 1.1 copy.542
  159.0 1.1 copy.540
  160.1 1.1 copy.543
  161.2 1.1 copy.544
  162.2 1.3 broadcast_multiply_fusion.8
  163.5 1.3 broadcast_multiply_fusion.9
  164.8 1.2 broadcast_multiply_fusion.6
  166.0 1.2 broadcast_multiply_fusion.10
  167.9 4.0 %pad_add_fusion = f32[16,3,512]{1,2,0:T(8,128)} fusion(f32[1,3,512]{1,2,0:T(8,128)S(1)} %get-tuple-element.273, f32[1,3,512]{1,2,0:T(8,128)S(1)} %get-tuple-element.274, f32[1,3,512]{1,2,0:T(8,128)S(1)} %get-tuple-element.275, f32[1,3,512]{1,2,0:T(8,128)S(1)} %get-tuple-element.276, f32[1,3,512]{1,2,0:T(8,128)S(1)} %get-tuple-element.277, ...), kind=kLoop, calls=%fused_computation.4 | loop fusion | flops 368640 | bytes 196608 | tf_op jit(solution)/shard_map/transpose(jvp())/add_any | solution.py:27
  172.3 2.8 %copy.504 = f32[16,3,512]{2,1,0:T(4,128)S(1)} copy(f32[16,3,512]{1,2,0:T(8,128)} %pad_add_fusion) | data formatting | bytes 196608 | tf_op jit(solution)/shard_map/transpose(jvp())/add_any | solution.py:27
  177.5 0.8 fusion.63
  180.2 7.7 %multiply_add_fusion.19 = (f32[1,512]{1,0:T(1,128)S(1)}, f32[1,512]{1,0:T(1,128)S(1)}, f32[1,512]{1,0:T(1,128)S(1)}, f32[1,512]{1,0:T(1,128)S(1)}, f32[1,512]{1,...) fusion(f32[1,512]{1,0:T(1,128)S(1)} %copy-done.12, f32[]{:T(128)} %bitcast.13, f32[]{:T(128)} %bitcast.15, ...), kind=kLoop, calls=%fused_computation.244 | loop fusion | flops 104960 | bytes 79924 | tf_op jit(solution)/shard_map/transpose(jvp())/add_any | solution.py:39
  187.9 3.7 %multiply_add_fusion.18 = (f32[1,512]{1,0:T(1,128)S(1)}, f32[1,512]{1,0:T(1,128)S(1)}) fusion(f32[1,512]{1,0:T(1,128)S(1)} %get-tuple-element.233, f32[1,512]{1,0:T(1,128)S(1)} %get-tuple-element.232, f32[1,512]{1,0:T(1,128)S(1)} %get-tuple-element.231, f32[1,512]{1,0:T(1,128)S(1)} %copy-done.11, f32[1,512]{1,0:T(1,128)S(1)} %get-tuple-element.228, ...), kind=kLoop, calls=%fused_computation.243 | loop fusion | flops 12800 | bytes 22552 | tf_op jit(solution)/shard_map/transpose(jvp())/add_any | solution.py:39
  192.1 33.3 %all_to_all.18 = f32[128,1,236]{2,1,0:T(1,128)S(1)} all-to-all(f32[128,1,236]{2,1,0:T(1,128)S(1)} %reshape.2686), channel_id=1, replica_groups=mesh['gauss'=128,'img'=4] {'gauss'}, dimensions={0} | all-to-all | bytes 241664 | tf_op jit(solution)/shard_map/all_to_all | solution.py:208
  225.4 0.9 reduce.27
  226.5 3.8 %scatter_custom_fusion.1 = f32[59,4096]{0,1:T(8,128)} fusion(s32[512]{0:T(512)} %bitcast.232, f32[512,59]{1,0:T(8,128)S(1)} %bitcast.211, f32[]{:T(128)} %constant.171.clone.1), kind=kCustom, calls=%fused_computation.20 | custom fusion | flops 30208 | bytes 967168 | tf_op jit(solution)/shard_map/scatter-add | solution.py:211
  230.9 28.1 %reduce-scatter.2.cloned.1.call-done = f32[59,1024]{0,1:T(8,128)} async-done(((f32[59,4096]{0,1:T(8,128)}), f32[59,1024]{0,1:T(8,128)}) %reduce-scatter.2.cloned.1.call-update) | async-done | bytes 241680 | tf_op jit(solution)/shard_map/reduce_scatter | solution.py:212
  259.0 1.9 copy.523
  (248 shorter events, 38.1 us)
Async XLA Ops:
  7.2 27.3 %copy-start.33 = (s32[1,2,256]{2,1,0:T(2,128)S(1)}, s32[1,2,256]{2,1,0:T(2,128)}, u32[]{:S(2)}) copy-start(s32[1,2,256]{2,1,0:T(2,128)} %param.11) | copy-start | bytes 6148
  7.2 27.9 %copy-start.66 = (s32[1,2]{1,0:T(1,128)S(1)}, s32[1,2]{1,0:T(1,128)}, u32[]{:S(2)}) copy-start(s32[1,2]{1,0:T(1,128)} %param.10) | copy-start | bytes 28
  7.2 28.5 %copy-start.8 = (f32[1,16]{1,0:T(1,128)S(1)}, f32[1,16]{1,0:T(1,128)}, u32[]{:S(2)}) copy-start(f32[1,16]{1,0:T(1,128)} %param.8) | copy-start | bytes 196
  14.0 39.9 %all-to-all-start = ((f32[128,1,236]{2,1,0:T(1,128)}), f32[128,1,236]{2,1,0:T(1,128)S(1)}, u32[]{:S(2)}, u32[]{:S(2)}) async-start(f32[128,1,236]{2,1,0:T(1,128)} %reshape.2684), calls=%async_computation | async-start | bytes 262144 | tf_op jit(solution)/shard_map/all_to_all | solution.py:205
  34.4 224.6 %reduce-scatter.2.cloned.1.call-start = ((), (), s32[]{:S(2)}) async-start(), calls=%async_computation.3 | async-start | bytes 2621440 | tf_op jit(solution)/shard_map/reduce_scatter | solution.py:212
  61.0 46.7 %copy-start.21 = (f32[1,512]{1,0:T(1,128)}, f32[1,512]{1,0:T(1,128)S(1)}, u32[]{:S(2)}) copy-start(f32[1,512]{1,0:T(1,128)S(1)} %slice.319) | copy-start | bytes 6148
  84.1 34.7 %copy-start = (f32[3,128,4]{0,2,1:T(4,128)S(1)}, f32[3,128,4]{0,2,1:T(4,128)}, u32[]{:S(2)}) copy-start(f32[3,128,4]{0,2,1:T(4,128)} %get-tuple-element.317) | copy-start | bytes 18436
  89.7 28.3 %copy-start.29 = (f32[1,512]{1,0:T(1,128)}, f32[1,512]{1,0:T(1,128)S(1)}, u32[]{:S(2)}) copy-start(f32[1,512]{1,0:T(1,128)S(1)} %slice.331) | copy-start | bytes 6148
  93.7 30.3 %copy-start.13 = (f32[1,512]{1,0:T(1,128)}, f32[1,512]{1,0:T(1,128)S(1)}, u32[]{:S(2)}) copy-start(f32[1,512]{1,0:T(1,128)S(1)} %reshape.2569) | copy-start | bytes 6148
  94.6 23.4 %copy-start.15 = (f32[1,512]{1,0:T(1,128)}, f32[1,512]{1,0:T(1,128)S(1)}, u32[]{:S(2)}) copy-start(f32[1,512]{1,0:T(1,128)S(1)} %reshape.2567) | copy-start | bytes 6148
  95.6 22.5 %copy-start.17 = (f32[1,512]{1,0:T(1,128)}, f32[1,512]{1,0:T(1,128)S(1)}, u32[]{:S(2)}) copy-start(f32[1,512]{1,0:T(1,128)S(1)} %add.2220) | copy-start | bytes 6148
  95.8 22.2 %copy-start.19 = (f32[1,512]{1,0:T(1,128)}, f32[1,512]{1,0:T(1,128)S(1)}, u32[]{:S(2)}) copy-start(f32[1,512]{1,0:T(1,128)S(1)} %reshape.2563) | copy-start | bytes 6148
  96.0 28.0 %copy-start.9 = (f32[1,512]{1,0:T(1,128)}, f32[1,512]{1,0:T(1,128)S(1)}, u32[]{:S(2)}) copy-start(f32[1,512]{1,0:T(1,128)S(1)} %div.905) | copy-start | bytes 6148
  102.6 16.2 %copy-start.25 = (f32[1,512]{1,0:T(1,128)}, f32[1,512]{1,0:T(1,128)S(1)}, u32[]{:S(2)}) copy-start(f32[1,512]{1,0:T(1,128)S(1)} %reshape.2565) | copy-start | bytes 6148
  105.0 19.0 %copy-start.39 = (s32[1024]{0:T(1024)S(1)}, s32[1024]{0:T(1024)}, u32[]{:S(2)}) copy-start(s32[1024]{0:T(1024)} %pad_clamp_fusion) | copy-start | bytes 12292
  106.8 20.0 %copy-start.62 = (pred[2,256]{1,0:T(4,128)(4,1)S(1)}, pred[2,256]{1,0:T(4,128)(4,1)}, u32[]{:S(2)}) copy-start(pred[2,256]{1,0:T(4,128)(4,1)} %compare_and_fusion.1) | copy-start | bytes 1540
  106.8 20.0 %copy-start.65 = (s32[1,2]{1,0:T(1,128)S(1)}, s32[1,2]{1,0:T(1,128)}, u32[]{:S(2)}) copy-start(s32[1,2]{1,0:T(1,128)} %param.12) | copy-start | bytes 28
  107.6 19.3 %copy-start.63 = (f32[2,256]{1,0:T(2,128)S(1)}, f32[2,256]{1,0:T(2,128)}, u32[]{:S(2)}) copy-start(f32[2,256]{1,0:T(2,128)} %get-tuple-element.403) | copy-start | bytes 6148
  107.6 19.3 %copy-start.64 = (f32[2,256]{1,0:T(2,128)S(1)}, f32[2,256]{1,0:T(2,128)}, u32[]{:S(2)}) copy-start(f32[2,256]{1,0:T(2,128)} %get-tuple-element.404) | copy-start | bytes 6148
  114.7 4.1 %copy-start.34 = (f32[1,512]{1,0:T(1,128)}, f32[1,512]{1,0:T(1,128)S(1)}, u32[]{:S(2)}) copy-start(f32[1,512]{1,0:T(1,128)S(1)} %get-tuple-element.243) | copy-start | bytes 6148
  122.0 9.4 %copy-start.38 = (f32[1,2,3,256]{3,1,2,0:T(2,128)S(1)}, f32[1,2,3,256]{3,1,2,0:T(2,128)}, u32[]{:S(2)}) copy-start(f32[1,2,3,256]{3,1,2,0:T(2,128)} %param.13) | copy-start | bytes 18436
  132.1 2.7 copy-start.5
  139.4 2.0 copy-start.1
  141.5 4.7 %copy-start.7 = (f32[128,4]{1,0:T(8,128)S(1)}, f32[128,4]{1,0:T(8,128)}, u32[]{:S(2)}) copy-start(f32[128,4]{1,0:T(8,128)} %get-tuple-element.323) | copy-start | bytes 6148
  171.9 3.3 %copy-start.35 = (f32[1,512]{1,0:T(1,128)S(1)}, f32[1,512]{1,0:T(1,128)}, u32[]{:S(2)}) copy-start(f32[1,512]{1,0:T(1,128)} %copy-done.34) | copy-start | bytes 6148
  171.9 3.3 %copy-start.36 = (f32[1,512]{1,0:T(1,128)S(1)}, f32[1,512]{1,0:T(1,128)}, u32[]{:S(2)}) copy-start(f32[1,512]{1,0:T(1,128)} %get-tuple-element.248) | copy-start | bytes 6148
  171.9 3.3 %copy-start.37 = (f32[1,512]{1,0:T(1,128)S(1)}, f32[1,512]{1,0:T(1,128)}, u32[]{:S(2)}) copy-start(f32[1,512]{1,0:T(1,128)} %get-tuple-element.262) | copy-start | bytes 6148
  171.9 5.5 %copy-start.22 = (f32[1,512]{1,0:T(1,128)S(1)}, f32[1,512]{1,0:T(1,128)}, u32[]{:S(2)}) copy-start(f32[1,512]{1,0:T(1,128)} %copy-done.21) | copy-start | bytes 6148
  171.9 5.5 %copy-start.23 = (f32[1,512]{1,0:T(1,128)S(1)}, f32[1,512]{1,0:T(1,128)}, u32[]{:S(2)}) copy-start(f32[1,512]{1,0:T(1,128)} %slice.324) | copy-start | bytes 6148
  171.9 5.5 %copy-start.24 = (f32[1,512]{1,0:T(1,128)S(1)}, f32[1,512]{1,0:T(1,128)}, u32[]{:S(2)}) copy-start(f32[1,512]{1,0:T(1,128)} %slice.322) | copy-start | bytes 6148
  172.0 5.5 %copy-start.27 = (f32[1,512]{1,0:T(1,128)S(1)}, f32[1,512]{1,0:T(1,128)}, u32[]{:S(2)}) copy-start(f32[1,512]{1,0:T(1,128)} %slice.329) | copy-start | bytes 6148
  172.0 5.5 %copy-start.28 = (f32[1,512]{1,0:T(1,128)S(1)}, f32[1,512]{1,0:T(1,128)}, u32[]{:S(2)}) copy-start(f32[1,512]{1,0:T(1,128)} %slice.333) | copy-start | bytes 6148
  172.0 5.5 %copy-start.30 = (f32[1,512]{1,0:T(1,128)S(1)}, f32[1,512]{1,0:T(1,128)}, u32[]{:S(2)}) copy-start(f32[1,512]{1,0:T(1,128)} %copy-done.29) | copy-start | bytes 6148
  172.0 5.5 %copy-start.31 = (f32[1,512]{1,0:T(1,128)S(1)}, f32[1,512]{1,0:T(1,128)}, u32[]{:S(2)}) copy-start(f32[1,512]{1,0:T(1,128)} %get-tuple-element.252) | copy-start | bytes 6148
  172.0 5.5 %copy-start.32 = (f32[1,512]{1,0:T(1,128)S(1)}, f32[1,512]{1,0:T(1,128)}, u32[]{:S(2)}) copy-start(f32[1,512]{1,0:T(1,128)} %get-tuple-element.271) | copy-start | bytes 6148
  172.0 5.5 %copy-start.58 = (f32[1,512]{1,0:T(1,128)S(1)}, f32[1,512]{1,0:T(1,128)}, u32[]{:S(2)}) copy-start(f32[1,512]{1,0:T(1,128)} %get-tuple-element.250) | copy-start | bytes 6148
  172.0 5.5 %copy-start.59 = (f32[1,512]{1,0:T(1,128)S(1)}, f32[1,512]{1,0:T(1,128)}, u32[]{:S(2)}) copy-start(f32[1,512]{1,0:T(1,128)} %get-tuple-element.251) | copy-start | bytes 6148
  172.0 5.5 %copy-start.60 = (f32[1,512]{1,0:T(1,128)S(1)}, f32[1,512]{1,0:T(1,128)}, u32[]{:S(2)}) copy-start(f32[1,512]{1,0:T(1,128)} %get-tuple-element.265) | copy-start | bytes 6148
  172.0 6.3 %copy-start.50 = (f32[512]{0:T(512)S(1)}, f32[512]{0:T(512)}, u32[]{:S(2)}) copy-start(f32[512]{0:T(512)} %sqrt.151) | copy-start | bytes 6148
  172.0 6.3 %copy-start.51 = (f32[512]{0:T(512)S(1)}, f32[512]{0:T(512)}, u32[]{:S(2)}) copy-start(f32[512]{0:T(512)} %squeeze.172) | copy-start | bytes 6148
  172.1 6.3 %copy-start.52 = (f32[512]{0:T(512)S(1)}, f32[512]{0:T(512)}, u32[]{:S(2)}) copy-start(f32[512]{0:T(512)} %squeeze.170) | copy-start | bytes 6148
  172.1 6.3 %copy-start.53 = (f32[512]{0:T(512)S(1)}, f32[512]{0:T(512)}, u32[]{:S(2)}) copy-start(f32[512]{0:T(512)} %squeeze.171) | copy-start | bytes 6148
  172.1 6.3 %copy-start.54 = (f32[512]{0:T(512)S(1)}, f32[512]{0:T(512)}, u32[]{:S(2)}) copy-start(f32[512]{0:T(512)} %squeeze.173) | copy-start | bytes 6148
  172.1 6.3 %copy-start.55 = (f32[512]{0:T(512)S(1)}, f32[512]{0:T(512)}, u32[]{:S(2)}) copy-start(f32[512]{0:T(512)} %squeeze.175) | copy-start | bytes 6148
  172.1 6.3 %copy-start.56 = (f32[512]{0:T(512)S(1)}, f32[512]{0:T(512)}, u32[]{:S(2)}) copy-start(f32[512]{0:T(512)} %squeeze.176) | copy-start | bytes 6148
  172.1 6.3 %copy-start.57 = (f32[512]{0:T(512)S(1)}, f32[512]{0:T(512)}, u32[]{:S(2)}) copy-start(f32[512]{0:T(512)} %squeeze.174) | copy-start | bytes 6148
  172.1 7.9 %copy-start.10 = (f32[1,512]{1,0:T(1,128)S(1)}, f32[1,512]{1,0:T(1,128)}, u32[]{:S(2)}) copy-start(f32[1,512]{1,0:T(1,128)} %sub.757) | copy-start | bytes 6148
  172.1 7.9 %copy-start.11 = (f32[1,512]{1,0:T(1,128)S(1)}, f32[1,512]{1,0:T(1,128)}, u32[]{:S(2)}) copy-start(f32[1,512]{1,0:T(1,128)} %sub.758) | copy-start | bytes 6148
  172.1 7.9 %copy-start.12 = (f32[1,512]{1,0:T(1,128)S(1)}, f32[1,512]{1,0:T(1,128)}, u32[]{:S(2)}) copy-start(f32[1,512]{1,0:T(1,128)} %sub.759) | copy-start | bytes 6148
  172.1 7.9 %copy-start.14 = (f32[1,512]{1,0:T(1,128)S(1)}, f32[1,512]{1,0:T(1,128)}, u32[]{:S(2)}) copy-start(f32[1,512]{1,0:T(1,128)} %copy-done.13) | copy-start | bytes 6148
  172.2 7.9 %copy-start.16 = (f32[1,512]{1,0:T(1,128)S(1)}, f32[1,512]{1,0:T(1,128)}, u32[]{:S(2)}) copy-start(f32[1,512]{1,0:T(1,128)} %copy-done.15) | copy-start | bytes 6148
  172.2 7.9 %copy-start.18 = (f32[1,512]{1,0:T(1,128)S(1)}, f32[1,512]{1,0:T(1,128)}, u32[]{:S(2)}) copy-start(f32[1,512]{1,0:T(1,128)} %copy-done.17) | copy-start | bytes 6148
  172.2 7.9 %copy-start.20 = (f32[1,512]{1,0:T(1,128)S(1)}, f32[1,512]{1,0:T(1,128)}, u32[]{:S(2)}) copy-start(f32[1,512]{1,0:T(1,128)} %copy-done.19) | copy-start | bytes 6148
  172.2 7.9 %copy-start.26 = (f32[1,512]{1,0:T(1,128)S(1)}, f32[1,512]{1,0:T(1,128)}, u32[]{:S(2)}) copy-start(f32[1,512]{1,0:T(1,128)} %copy-done.25) | copy-start | bytes 6148
  172.2 7.9 %copy-start.40 = (f32[512]{0:T(512)S(1)}, f32[512]{0:T(512)}, u32[]{:S(2)}) copy-start(f32[512]{0:T(512)} %get-tuple-element.142) | copy-start | bytes 6148
  172.2 7.9 %copy-start.41 = (f32[512]{0:T(512)S(1)}, f32[512]{0:T(512)}, u32[]{:S(2)}) copy-start(f32[512]{0:T(512)} %get-tuple-element.144) | copy-start | bytes 6148
  172.2 7.9 %copy-start.42 = (f32[512]{0:T(512)S(1)}, f32[512]{0:T(512)}, u32[]{:S(2)}) copy-start(f32[512]{0:T(512)} %get-tuple-element.145) | copy-start | bytes 6148
  172.2 7.9 %copy-start.43 = (f32[512]{0:T(512)S(1)}, f32[512]{0:T(512)}, u32[]{:S(2)}) copy-start(f32[512]{0:T(512)} %get-tuple-element.147) | copy-start | bytes 6148
  172.2 7.9 %copy-start.44 = (f32[512]{0:T(512)S(1)}, f32[512]{0:T(512)}, u32[]{:S(2)}) copy-start(f32[512]{0:T(512)} %get-tuple-element.148) | copy-start | bytes 6148
  172.2 7.9 %copy-start.45 = (f32[512]{0:T(512)S(1)}, f32[512]{0:T(512)}, u32[]{:S(2)}) copy-start(f32[512]{0:T(512)} %get-tuple-element.149) | copy-start | bytes 6148
  172.3 7.9 %copy-start.46 = (f32[512]{0:T(512)S(1)}, f32[512]{0:T(512)}, u32[]{:S(2)}) copy-start(f32[512]{0:T(512)} %get-tuple-element.150) | copy-start | bytes 6148
  172.3 7.9 %copy-start.47 = (f32[512]{0:T(512)S(1)}, f32[512]{0:T(512)}, u32[]{:S(2)}) copy-start(f32[512]{0:T(512)} %get-tuple-element.151) | copy-start | bytes 6148
  172.3 7.9 %copy-start.48 = (f32[512]{0:T(512)S(1)}, f32[512]{0:T(512)}, u32[]{:S(2)}) copy-start(f32[512]{0:T(512)} %get-tuple-element.152) | copy-start | bytes 6148
  172.3 7.9 %copy-start.49 = (f32[512]{0:T(512)S(1)}, f32[512]{0:T(512)}, u32[]{:S(2)}) copy-start(f32[512]{0:T(512)} %get-tuple-element.153) | copy-start | bytes 6148
  (5 other events, 8.7 us)
Sparse Core Ops, SparseCore 0:
  230.4 28.5 reduce-scatter.1
where the time goes:
time: 270 us; the launch traced here: 268 us
  other arithmetic  80.2 us (30%)
  local copies, waits for them, and re-layouts  68.2 us (25%)
  blocking collectives  33.3 us (12%)
  between operations  31.7 us (12%)
  waiting for transfers between devices  28.1 us (10%)
  starting transfers between devices  20.4 us (8%)
  matrix products  5.85 us (2%)
    all_to_all x1, blocking collectives, local(): lax.all_to_all(pullback(grad_feats)[0], 'gauss', split_axis=1, concat_axi...  33.3 us
    reduce_scatter x1, waiting for transfers between devices, local(): summed = lax.psum_scatter(local_sum, 'img', scatter_dimension=1, tiled=True)  28.1 us
    all_to_all x1, starting transfers between devices, local(): lax.all_to_all(outgoing, 'gauss', split_axis=1, concat_axis=1, tiled=True)  20.4 us
    add x3, other arithmetic, project(): jacobian[a][0] * rotation[0][j] + jacobian[a][1] * rotation[1][j]  16.9 us
    unnamed x162, local copies, waits for them, and re-layouts  15.4 us
    add x12, local copies, waits for them, and re-layouts, project(): jacobian[a][0] * rotation[0][j] + jacobian[a][1] * rotation[1][j]  8.75 us
    add_any x1, other arithmetic, project(): rotation[i][2] * world[2]  7.71 us
    div x1, other arithmetic, project(): cov_xx / determ  7.04 us
  transfers between devices with their start and end apart: 2, of which 1 were waited for; matrix products, arithmetic and copies ran while one was open for 1% of the time, Pallas kernels for 0%

commit v1 on v0

v1 whole, which is shorter than its diff:
```python
import jax
import jax.numpy as jnp
from jax import lax
from jax.experimental import pallas as pl
from jax.experimental.pallas import tpu as pltpu
from jax.sharding import PartitionSpec as P

MESH = pl.DeviceIdType.MESH
F32 = jnp.float32
BF16 = jnp.bfloat16
HIGHEST = lax.Precision.HIGHEST

FEATS = 9
PARAMS = 59
G_DEV = 4096
QUARTER = 1024
ROWS = 512
LIST = 256

sh_zero = 0.28209479177387814
sh_one = 0.4886025119029199
sh_two = [1.0925484305920792, -1.0925484305920792, 0.31539156525252005, -1.0925484305920792, 0.5462742152960396]
sh_three = [
    -0.5900435899266435,
    2.890611442640554,
    -0.4570457994644658,
    0.3731763325901154,
    -0.4570457994644658,
    1.445305721320277,
    -0.5900435899266435,
]


def project_rows(rows, camera):
    m = rows[0:3]
    rot = [[camera[3 * i + j] for j in range(3)] for i in range(3)]
    shift = camera[9:12]
    focal_x, focal_y, centre_x, centre_y = camera[12:16]
    p = [rot[i][0] * m[0] + rot[i][1] * m[1] + rot[i][2] * m[2] + shift[i] for i in range(3)]
    inv_z = 1.0 / p[2]
    xn, yn = p[0] * inv_z, p[1] * inv_z
    u = focal_x * xn + centre_x
    v = focal_y * yn + centre_y
    jx, jy = focal_x * inv_z, focal_y * inv_z
    q = rows[6:10]
    inv_q = 1.0 / jnp.sqrt(q[0] * q[0] + q[1] * q[1] + q[2] * q[2] + q[3] * q[3])
    w, x, y, z = (t * inv_q for t in q)
    rg = [
        [1.0 - 2.0 * (y * y + z * z), 2.0 * (x * y - w * z), 2.0 * (x * z + w * y)],
        [2.0 * (x * y + w * z), 1.0 - 2.0 * (x * x + z * z), 2.0 * (y * z - w * x)],
        [2.0 * (x * z - w * y), 2.0 * (y * z + w * x), 1.0 - 2.0 * (x * x + y * y)],
    ]
    scales = [jnp.exp(rows[3 + k]) for k in range(3)]
    sx = [jx * (rot[0][j] - xn * rot[2][j]) for j in range(3)]
    sy = [jy * (rot[1][j] - yn * rot[2][j]) for j in range(3)]
    bx = [(sx[0] * rg[0][k] + sx[1] * rg[1][k] + sx[2] * rg[2][k]) * scales[k] for k in range(3)]
    by = [(sy[0] * rg[0][k] + sy[1] * rg[1][k] + sy[2] * rg[2][k]) * scales[k] for k in range(3)]
    cxx = bx[0] * bx[0] + bx[1] * bx[1] + bx[2] * bx[2] + 0.3
    cxy = bx[0] * by[0] + bx[1] * by[1] + bx[2] * by[2]
    cyy = by[0] * by[0] + by[1] * by[1] + by[2] * by[2] + 0.3
    inv_det = 1.0 / (cxx * cyy - cxy * cxy)
    opacity = 1.0 / (1.0 + jnp.exp(-rows[10]))
    view = [m[j] + (rot[0][j] * shift[0] + rot[1][j] * shift[1] + rot[2][j] * shift[2]) for j in range(3)]
    inv_len = 1.0 / jnp.sqrt(view[0] * view[0] + view[1] * view[1] + view[2] * view[2])
    dx, dy, dz = (t * inv_len for t in view)
    xx, yy, zz = dx * dx, dy * dy, dz * dz
    basis = [
        -sh_one * dy,
        sh_one * dz,
        -sh_one * dx,
        sh_two[0] * dx * dy,
        sh_two[1] * dy * dz,
        sh_two[2] * (2.0 * zz - xx - yy),
        sh_two[3] * dx * dz,
        sh_two[4] * (xx - yy),
        sh_three[0] * dy * (3.0 * xx - yy),
        sh_three[1] * dx * dy * dz,
        sh_three[2] * dy * (4.0 * zz - xx - yy),
        sh_three[3] * dz * (2.0 * zz - 3.0 * xx - 3.0 * yy),
        sh_three[4] * dx * (4.0 * zz - xx - yy),
        sh_three[5] * dz * (xx - yy),
        sh_three[6] * dx * (xx - 3.0 * yy),
    ]
    colour = []
    for c in range(3):
        total = 0.5 + sh_zero * rows[11 + c]
        for k in range(1, 16):
            total = total + basis[k - 1] * rows[11 + 3 * k + c]
        colour.append(total)
    return [u, v, cyy * inv_det, -cxy * inv_det, cxx * inv_det, *colour, opacity]


def split(value, parts):
    out = []
    for _ in range(parts - 1):
        piece = value.astype(BF16)
        out.append(piece)
        value = value - piece.astype(F32)
    out.append(value.astype(BF16))
    return out


def dot_nn(a, b, precision=None):
    return lax.dot_general(a, b, (((1,), (0,)), ((), ())), precision=precision, preferred_element_type=F32)


def dot_nt(a, b, precision=None):
    return lax.dot_general(a, b, (((1,), (1,)), ((), ())), precision=precision, preferred_element_type=F32)


def where_equal(a, b):
    return jnp.where(a == b, 1.0, 0.0).astype(BF16)


def iota(shape, dim):
    return lax.broadcasted_iota(jnp.int32, shape, dim)


def place(x, z, c):
    return (x * 16 + z) * 2 + c


def as_message(feats):
    blocks = [feats[:, k * 128 : (k + 1) * 128] for k in range(4)]
    both = jnp.concatenate(blocks + blocks, axis=0).T
    return jnp.where(iota((64, 128), 1) < 64, both[0:64], both[64:128])


def kernel(
    params,
    cam,
    send_rows,
    tiles,
    lists,
    counts,
    targets,
    grads,
    rendered,
    pv,
    tail,
    pq,
    gq,
    camx,
    p3,
    oh,
    gs,
    fs,
    msg,
    mid,
    got,
    turned,
    ohr,
    upper,
    lower,
    fe,
    al,
    lk,
    bf,
    ws,
    sw2,
    rs,
    rt,
    ge,
    st,
    sv,
    psem,
    qsem,
    osem,
    csend,
    crecv,
    zsend,
    zrecv,
    xsend,
    xrecv,
    ysend,
    yrecv,
):
    me, my = lax.axis_index("gauss"), lax.axis_index("img")
    mx, mz, mc = me // 32, (me // 2) % 16, me % 2
    far_first = [8, 7, 9, 6, 10, 5, 11, 4, 12, 3, 13, 2, 14, 1, 15]
    z_peers = [(mz + j) % 16 for j in far_first]
    x_peers = [((mx + j // 2) % 4, (mc + j) % 2) for j in (4, 5, 2, 3, 6, 7, 1)]
    y_peers = [(my + j) % 4 for j in (2, 1, 3)]

    barrier = pltpu.get_barrier_semaphore()
    for z in z_peers:
        pl.semaphore_signal(barrier, inc=1, device_id={"gauss": place(mx, z, mc)}, device_id_type=MESH)
    for x, c in x_peers:
        pl.semaphore_signal(barrier, inc=1, device_id={"gauss": place(x, mz, c)}, device_id_type=MESH)
    for y in y_peers:
        pl.semaphore_signal(barrier, inc=1, device_id={"img": y}, device_id_type=MESH)

    load = pltpu.make_async_copy(params, pv, psem)
    load.start()
    for block in range(8):
        columns = pl.ds(pl.multiple_of(my * QUARTER + block * 128, 128), 128)
        pltpu.make_async_copy(params.at[:, columns], pq.at[block], qsem).start()

    for k in range(16):
        camx[my, k : k + 1, :] = jnp.zeros((1, 128), F32) + cam[0, k]

    sent = send_rows[...]
    row = iota((16, ROWS), 0)
    pieces = jnp.where(row == 0, (sent >> 6).astype(F32), jnp.where(row == 1, (sent & 63).astype(F32), 0.0))
    column = iota((ROWS, ROWS), 1)
    natural = ((column & 63) << 3) | (((column >> 6) & 1) << 2) | (column >> 7)
    order = where_equal(iota((ROWS, ROWS), 0), natural)
    pieces = dot_nn(pieces.astype(BF16), order)
    chosen = pieces[0:1] * 64.0 + pieces[1:2]

    @pl.loop(0, 64)
    def _(j):
        start = pl.multiple_of(j * 64, 64)
        gauss = (iota((64, ROWS), 0) + start).astype(F32)
        oh[pl.ds(start, 64), :] = where_equal(gauss, chosen)

    tail[...] = jnp.zeros((8, G_DEV), F32)
    load.wait()

    @pl.loop(0, 16)
    def _(j):
        here = pl.ds(pl.multiple_of(j * 256, 256), 256)
        tail[0:3, here] = pv[56:PARAMS, here]
        whole = jnp.concatenate([pv[0:56, here], tail[:, here]], axis=0)
        for n, piece in enumerate(split(whole, 3)):
            p3[64 * n : 64 * (n + 1), here] = piece

    picked = dot_nn(p3[...], oh[...])
    gs[...] = picked[0:64] + picked[64:128] + picked[128:192]
    feats = project_rows([gs[f : f + 1, :] for f in range(PARAMS)], [cam[0, k] for k in range(16)])
    fs[8:16, :] = jnp.zeros((8, ROWS), F32)
    for f in range(FEATS):
        fs[f : f + 1, :] = feats[f]

    pl.semaphore_wait(barrier, 25)

    for n, y in enumerate(y_peers):
        pltpu.make_async_remote_copy(
            src_ref=camx.at[my], dst_ref=camx.at[my], send_sem=csend.at[n], recv_sem=crecv.at[n],
            device_id={"img": y}, device_id_type=MESH,
        ).start()

    def exchange(turn, while_sent):
        z_copies, x_copies = [], []
        for z in z_peers:
            copy = pltpu.make_async_remote_copy(
                src_ref=msg.at[turn, :, z], dst_ref=mid.at[turn, mz], send_sem=zsend.at[turn], recv_sem=zrecv.at[turn],
                device_id={"gauss": place(mx, z, mc)}, device_id_type=MESH,
            )
            copy.start()
        mid[turn, mz] = msg[turn, :, mz]
        while_sent()
        span = mid.at[turn, pl.ds(0, 15)]
        pltpu.make_async_copy(span, span, zrecv.at[turn]).wait()
        mine = mc * 4 + mx
        for x, c in x_peers:
            pltpu.make_async_remote_copy(
                src_ref=mid.at[turn, :, x], dst_ref=got.at[turn, mine], send_sem=xsend.at[turn], recv_sem=xrecv.at[turn],
                device_id={"gauss": place(x, mz, c)}, device_id_type=MESH,
            ).start()
        got[turn, mine] = mid[turn, :, mx]
        pltpu.make_async_copy(span, span, zsend.at[turn]).wait()
        span = got.at[turn, pl.ds(0, 7)]
        pltpu.make_async_copy(span, span, xrecv.at[turn]).wait()
        pltpu.make_async_copy(span, span, xsend.at[turn]).wait()
        turned[...] = got.reshape(256, 128)[turn * 128 : (turn + 1) * 128, :].T
        half = turned[pl.ds(pl.multiple_of(mc * 64, 64), 64), :]
        return jnp.concatenate([half[16 * k : 16 * (k + 1)] for k in range(4)], axis=1)

    def prepare():
        named = jnp.concatenate([lists[0, 0:1, :], lists[0, 1:2, :]], axis=1)
        named = ((named & 3) << 7) | (((named >> 2) & 1) << 6) | (named >> 3)

        @pl.loop(0, 8)
        def _(j):
            start = pl.multiple_of(j * 64, 64)
            ohr[pl.ds(start, 64), :] = where_equal(iota((64, ROWS), 0) + start, named)

        earlier = jnp.where(iota((LIST, LIST), 0) < iota((LIST, LIST), 1), 1.0, 0.0).astype(BF16)
        for n in range(3):
            upper[LIST * n : LIST * (n + 1), :] = earlier
        later = jnp.where(iota((LIST, LIST), 0) > iota((LIST, LIST), 1), 1.0, 0.0).astype(BF16)
        for n in range(2):
            lower[LIST * n : LIST * (n + 1), :] = later

    msg.reshape(128, 128)[0:64, :] = as_message(fs[...])
    received = exchange(0, prepare)

    listed = dot_nn(jnp.concatenate(split(received, 3), axis=0), ohr[...])
    fe[...] = listed[0:16] + listed[16:32] + listed[32:48]

    def entry(f, t):
        return fe[f : f + 1, t * LIST : (t + 1) * LIST]

    pixel = iota((16, LIST), 0).astype(F32)
    off_x, quad_x, cross, quad_y, origin_y, weight = [], [], [], [], [], []
    for t in range(2):
        tile = tiles[0, t]
        off_x.append(entry(0, t) - (pixel + ((tile & 15) * 16).astype(F32)))
        origin_y.append(entry(1, t) - ((tile >> 4) * 16).astype(F32))
        quad_x.append(-0.5 * entry(2, t) * off_x[t] * off_x[t])
        cross.append(-entry(3, t))
        quad_y.append(-0.5 * entry(4, t))
        weight.append(jnp.where(iota((1, LIST), 1) < counts[0, t], entry(8, t), 0.0))

    def pixels(t, j):
        return pl.ds(pl.multiple_of(t * 256 + j * 16, 16), 16)

    @pl.loop(0, 16)
    def _(j):
        for t in range(2):
            here = pixels(t, j)
            off_y = origin_y[t] - j.astype(F32)
            power = quad_x[t] + off_x[t] * (cross[t] * off_y) + quad_y[t] * off_y * off_y
            alpha = weight[t] * jnp.exp(power)
            al[here, :] = alpha
            for n, piece in enumerate(split(jnp.log(1.0 - alpha), 3)):
                lk[here, LIST * n : LIST * (n + 1)] = piece

    bf[...] = dot_nn(lk[...], upper[...])

    @pl.loop(0, 16)
    def _(j):
        for t in range(2):
            here = pixels(t, j)
            ws[here, :] = al[here, :] * jnp.exp(bf[here, :])

    grad_colour = []
    for t in range(2):
        shown = ws[t * 256 : (t + 1) * 256, :]
        colours = dot_nt(fe[:, t * LIST : (t + 1) * LIST], shown, HIGHEST)[5:8]
        rendered[0, t] = colours
        rs[t] = jnp.zeros((8, 256), F32)
        rs[t, 0:3, :] = colours - targets[0, t]
        rt[t * 256 : (t + 1) * 256, :] = rs[t].T
        grad_colour.append(dot_nn(rs[t], shown, HIGHEST))

    @pl.loop(0, 16)
    def _(j):
        for t in range(2):
            here = pixels(t, j)
            resid = rt[here, :]
            along = resid[:, 0:1] * entry(5, t) + resid[:, 1:2] * entry(6, t) + resid[:, 2:3] * entry(7, t)
            share = along * ws[here, :]
            ws[here, :] = share
            for n, piece in enumerate(split(share, 2)):
                sw2[here, LIST * n : LIST * (n + 1)] = piece

    bf[...] = dot_nn(sw2[...], lower[...])

    ge[8:16, :] = jnp.zeros((8, ROWS), F32)
    for t in range(2):

        def moments(j, carry):
            here = pixels(t, j)
            alpha = al[here, :]
            off_y = origin_y[t] - j.astype(F32)
            flow = ws[here, :] - bf[here, :] * (alpha / (1.0 - alpha))
            flow_y = flow * off_y
            return carry[0] + flow, carry[1] + flow_y, carry[2] + flow_y * off_y

        zero = jnp.zeros((16, LIST), F32)
        flow, flow_y, flow_yy = lax.fori_loop(0, 16, moments, (zero, zero, zero))

        def over(value):
            return jnp.sum(value, axis=0, keepdims=True)

        m_x, m_y = over(flow * off_x[t]), over(flow_y)
        a, b, c = entry(2, t), entry(3, t), entry(4, t)
        out = [
            -(a * m_x + b * m_y),
            -(b * m_x + c * m_y),
            -0.5 * over(flow * off_x[t] * off_x[t]),
            -over(flow_y * off_x[t]),
            -0.5 * over(flow_yy),
            grad_colour[t][0:1],
            grad_colour[t][1:2],
            grad_colour[t][2:3],
            over(flow) / entry(8, t),
        ]
        for f in range(FEATS):
            ge[f : f + 1, t * LIST : (t + 1) * LIST] = out[f]

    back = dot_nt(jnp.concatenate(split(ge[...], 2), axis=0), ohr[...])
    msg.reshape(128, 128)[64:128, :] = as_message(back[0:16] + back[16:32])
    returned = exchange(1, lambda: None)
    returned = jnp.concatenate(split(returned, 2), axis=0)

    for n, q in enumerate(y_peers + [my]):
        part = dot_nt(returned, oh[pl.ds(pl.multiple_of(q * QUARTER, QUARTER), QUARTER), :])
        part = part[0:16] + part[16:32]
        for block in range(8):
            value = part[0:FEATS, block * 128 : (block + 1) * 128]
            if n < 3:
                st[n, :, block, :] = value
            else:
                sv[my, :, block, :] = value
        if n < 3:
            pltpu.make_async_remote_copy(
                src_ref=st.at[n], dst_ref=sv.at[my], send_sem=ysend.at[n], recv_sem=yrecv.at[n],
                device_id={"img": q}, device_id_type=MESH,
            ).start()

    pltpu.make_async_copy(pq, pq, qsem).wait()
    for n in range(3):
        pltpu.make_async_copy(camx.at[0], camx.at[0], csend.at[n]).wait()
        pltpu.make_async_copy(camx.at[0], camx.at[0], crecv.at[n]).wait()
    gq[...] = jnp.zeros((8, PARAMS, 128), F32)
    for n in range(3):
        pltpu.make_async_copy(st.at[n], st.at[n], yrecv.at[n]).wait()

    @pl.loop(0, 4)
    def _(view):
        camera = [jnp.broadcast_to(camx[view, k : k + 1, :], (8, 128)) for k in range(16)]
        _, pull = jax.vjp(lambda rows: project_rows(rows, camera), [pq[:, f, :] for f in range(PARAMS)])
        (out,) = pull([sv[view, f] for f in range(FEATS)])
        for f in range(PARAMS):
            gq[:, f, :] += out[f]

    for block in range(8):
        pltpu.make_async_copy(gq.at[block], grads.at[:, pl.ds(block * 128, 128)], osem).start()
    for n in range(3):
        pltpu.make_async_copy(st.at[n], st.at[n], ysend.at[n]).wait()
    pltpu.make_async_copy(gq, gq, osem).wait()


def local(params, cameras, send_rows, tile_ids, lists, counts, targets):
    vmem, smem, hbm = (pl.BlockSpec(memory_space=s) for s in (pltpu.VMEM, pltpu.SMEM, pl.ANY))
    dma = pltpu.SemaphoreType.DMA
    return pl.pallas_call(
        kernel,
        out_shape=(
            jax.ShapeDtypeStruct((PARAMS, QUARTER), F32),
            jax.ShapeDtypeStruct((1, 2, 3, 256), F32),
        ),
        in_specs=[hbm, smem, vmem, smem, vmem, smem, vmem],
        out_specs=(hbm, vmem),
        scratch_shapes=[
            pltpu.VMEM((PARAMS, G_DEV), F32),
            pltpu.VMEM((8, G_DEV), F32),
            pltpu.VMEM((8, PARAMS, 128), F32),
            pltpu.VMEM((8, PARAMS, 128), F32),
            pltpu.VMEM((4, 16, 128), F32),
            pltpu.VMEM((192, G_DEV), BF16),
            pltpu.VMEM((G_DEV, ROWS), BF16),
            pltpu.VMEM((64, ROWS), F32),
            pltpu.VMEM((16, ROWS), F32),
            pltpu.VMEM((2, 4, 16, 1, 128), F32),
            pltpu.VMEM((2, 16, 4, 1, 128), F32),
            pltpu.VMEM((2, 8, 16, 1, 128), F32),
            pltpu.VMEM((128, 128), F32),
            pltpu.VMEM((ROWS, ROWS), BF16),
            pltpu.VMEM((3 * LIST, LIST), BF16),
            pltpu.VMEM((2 * LIST, LIST), BF16),
            pltpu.VMEM((16, ROWS), F32),
            pltpu.VMEM((512, LIST), F32),
            pltpu.VMEM((512, 3 * LIST), BF16),
            pltpu.VMEM((512, LIST), F32),
            pltpu.VMEM((512, LIST), F32),
            pltpu.VMEM((512, 2 * LIST), BF16),
            pltpu.VMEM((2, 8, 256), F32),
            pltpu.VMEM((512, 8), F32),
            pltpu.VMEM((16, ROWS), F32),
            pltpu.VMEM((3, FEATS, 8, 128), F32),
            pltpu.VMEM((4, FEATS, 8, 128), F32),
            dma,
            dma,
            dma,
            dma((3,)),
            dma((3,)),
            dma((2,)),
            dma((2,)),
            dma((2,)),
            dma((2,)),
            dma((3,)),
            dma((3,)),
        ],
        compiler_params=pltpu.CompilerParams(
            collective_id=0, has_side_effects=True, vmem_limit_bytes=40 * 1024 * 1024
        ),
    )(params, cameras, send_rows, tile_ids, lists, counts, targets)


def solution(mesh):
    placed = (
        P(None, "gauss"),
        P("img", None),
        P("img", "gauss"),
        P("img", "gauss"),
        P("img", "gauss", None),
        P("img", "gauss"),
        P("img", "gauss", None, None),
    )
    return jax.shard_map(
        local,
        mesh=mesh,
        in_specs=placed,
        out_specs=(P(None, ("gauss", "img")), P("img", "gauss", None, None)),
        check_vma=False,
    )
```

time: 270 us -> 56.4 us (0.21)
  other arithmetic: 80.2 us -> 0 us
  local copies, waits for them, and re-layouts: 68.2 us -> 3.26 us
  Pallas kernels: 0 us -> 52.2 us
  blocking collectives: 33.3 us -> 0 us
  between operations: 31.7 us -> 0.71 us
  waiting for transfers between devices: 28.1 us -> 0 us
  starting transfers between devices: 20.4 us -> 0 us
  matrix products: 5.85 us -> 0 us
    pallas_call x0 -> x1, Pallas kernels: none -> 52.2 us  [local(): pl.pallas_call(kernel, out_shape=(jax.ShapeDtypeStruct((PARAMS, QUARTER),...]
    all_to_all x1 -> x0, blocking collectives: 33.3 us -> none  [local(): lax.all_to_all(pullback(grad_feats)[0], 'gauss', split_axis=1, concat_axi...]
    reduce_scatter x1 -> x0, waiting for transfers between devices: 28.1 us -> none  [local(): summed = lax.psum_scatter(local_sum, 'img', scatter_dimension=1, tiled=True)]
    all_to_all x1 -> x0, starting transfers between devices: 20.4 us -> none  [local(): lax.all_to_all(outgoing, 'gauss', split_axis=1, concat_axis=1, tiled=True)]
    add x4 -> x0, other arithmetic: 20.2 us -> none  [the longest x3 16.9 us: project(): jacobian[a][0] * rotation[0][j] + jacobian[a][1] * rotation[1][j]]
    add_any x6 -> x0, other arithmetic: 16.3 us -> none  [the longest x1 7.71 us: project(): rotation[i][2] * world[2]]
    unnamed x162 -> x14, local copies, waits for them, and re-layouts: 15.4 us -> 2.67 us
    add x16 -> x0, local copies, waits for them, and re-layouts: 12.1 us -> none  [the longest x12 8.75 us: project(): jacobian[a][0] * rotation[0][j] + jacobian[a][1] * rotation[1][j]]
  transfers between devices with their start and end apart: 2 -> 0, of which waited for: 1 -> 0; matrix products, arithmetic and copies ran while one was open for 1% -> 0% of each run, Pallas kernels for 0% -> 0%
where the time goes in v1:
time: 56.4 us; the launch traced here: 56.2 us
  Pallas kernels  52.2 us (93%)
  local copies, waits for them, and re-layouts  3.26 us (6%)
  between operations  0.71 us (1%)
    pallas_call x1, Pallas kernels, local(): pl.pallas_call(kernel, out_shape=(jax.ShapeDtypeStruct((PARAMS, QUARTER),...  52.2 us
    unnamed x14, local copies, waits for them, and re-layouts  2.67 us

profile of v1, /device:TPU:1, one launch (start us, length us, event | category | flops | bytes accessed | tf_op | source)
XLA Modules:
  0.0 56.2 jit_solution(3955794922425853174)
XLA Ops:
  0.6 0.0 copy-start.5
  0.6 0.0 copy-start.2
  0.7 0.0 copy-start.4
  0.7 0.0 copy-start.1
  0.7 0.0 copy-start.3
  0.7 0.7 %copy.9.targets = f32[1,2,3,256]{3,2,1,0:T(4,128)S(1)} copy(f32[1,2,3,256]{3,1,2,0:T(2,128)} %param.13) | data formatting | bytes 12288 | tf_op args[6]
  1.4 0.0 copy-done.5
  1.4 0.0 copy-done.2
  1.4 0.0 copy-done.4
  1.4 0.0 copy-done.1
  1.4 0.0 copy-done.3
  1.4 0.0 copy-start
  1.4 1.2 %copy-done = f32[59,4096]{1,0:T(8,128)S(1)} copy-done((f32[59,4096]{1,0:T(8,128)S(1)}, f32[59,4096]{1,0:T(8,128)}, u32[]{:S(2)}) %copy-start) | copy-done | bytes 966680
  2.7 52.2 %shard_map.86 = (f32[59,1024]{1,0:T(8,128)S(1)}, f32[1,2,3,256]{3,2,1,0:T(4,128)S(1)}) custom-call(f32[59,4096]{1,0:T(8,128)S(1)} %copy-done, f32[1,16]{1,0:T(1,128)S(1)} %copy-done.3, s32[1,512]{1,0:T(1,128)S(1)} %copy-done.1, s32[1,2]{1,0:T(1,128)S(1)} %copy-done.4, s32[1,2,256]{2,1,0:T(2,128)S(1)} %copy-done.2, s32[1,2]{1,0:T(1,128)S(1)} %copy-done.5, ...), custom_call_target="tpu_custom_call" | custom-call | tf_op jit(solution)/shard_map/pallas_call | solution.py:430
  54.9 0.6 %copy.10 = f32[1,2,3,256]{3,1,2,0:T(2,128)} copy(f32[1,2,3,256]{3,2,1,0:T(4,128)S(1)} %get-tuple-element.3) | data formatting | bytes 12288 | tf_op jit(solution)/shard_map/pallas_call | solution.py:430
  55.5 0.7 %copy.12 = f32[59,1024]{1,0:T(8,128)} copy(f32[59,1024]{1,0:T(8,128)S(1)} %get-tuple-element.6) | data formatting | bytes 483328
Async XLA Ops:
  0.6 0.8 %copy-start.5 = (s32[1,2]{1,0:T(1,128)S(1)}, s32[1,2]{1,0:T(1,128)}, u32[]{:S(2)}) copy-start(s32[1,2]{1,0:T(1,128)} %counts.1) | copy-start | bytes 28
  0.6 0.8 %copy-start.2 = (s32[1,2,256]{2,1,0:T(2,128)S(1)}, s32[1,2,256]{2,1,0:T(2,128)}, u32[]{:S(2)}) copy-start(s32[1,2,256]{2,1,0:T(2,128)} %lists.1) | copy-start | bytes 6148
  0.7 0.8 %copy-start.4 = (s32[1,2]{1,0:T(1,128)S(1)}, s32[1,2]{1,0:T(1,128)}, u32[]{:S(2)}) copy-start(s32[1,2]{1,0:T(1,128)} %tiles.1) | copy-start | bytes 28
  0.7 0.8 %copy-start.1 = (s32[1,512]{1,0:T(1,128)S(1)}, s32[1,512]{1,0:T(1,128)}, u32[]{:S(2)}) copy-start(s32[1,512]{1,0:T(1,128)} %send_rows.1) | copy-start | bytes 6148
  0.7 0.8 %copy-start.3 = (f32[1,16]{1,0:T(1,128)S(1)}, f32[1,16]{1,0:T(1,128)}, u32[]{:S(2)}) copy-start(f32[1,16]{1,0:T(1,128)} %cam.1) | copy-start | bytes 196
  1.4 1.2 %copy-start = (f32[59,4096]{1,0:T(8,128)S(1)}, f32[59,4096]{1,0:T(8,128)}, u32[]{:S(2)}) copy-start(f32[59,4096]{1,0:T(8,128)} %params.1) | copy-start | bytes 2899972

commit v2 on v1

v2 whole, which is shorter than its diff:
```python
import jax
import jax.numpy as jnp
from jax import lax
from jax.experimental import pallas as pl
from jax.experimental.pallas import tpu as pltpu
from jax.sharding import PartitionSpec as P

MESH = pl.DeviceIdType.MESH
F32 = jnp.float32
BF16 = jnp.bfloat16
HIGHEST = lax.Precision.HIGHEST

FEATS = 9
PARAMS = 59
G_DEV = 4096
QUARTER = 1024
ROWS = 512
LIST = 256

sh_zero = 0.28209479177387814
sh_one = 0.4886025119029199
sh_two = [1.0925484305920792, -1.0925484305920792, 0.31539156525252005, -1.0925484305920792, 0.5462742152960396]
sh_three = [
    -0.5900435899266435,
    2.890611442640554,
    -0.4570457994644658,
    0.3731763325901154,
    -0.4570457994644658,
    1.445305721320277,
    -0.5900435899266435,
]


def project_rows(rows, camera):
    m = rows[0:3]
    rot = [[camera[3 * i + j] for j in range(3)] for i in range(3)]
    shift = camera[9:12]
    focal_x, focal_y, centre_x, centre_y = camera[12:16]
    p = [rot[i][0] * m[0] + rot[i][1] * m[1] + rot[i][2] * m[2] + shift[i] for i in range(3)]
    inv_z = 1.0 / p[2]
    xn, yn = p[0] * inv_z, p[1] * inv_z
    u = focal_x * xn + centre_x
    v = focal_y * yn + centre_y
    jx, jy = focal_x * inv_z, focal_y * inv_z
    q = rows[6:10]
    inv_q = 1.0 / jnp.sqrt(q[0] * q[0] + q[1] * q[1] + q[2] * q[2] + q[3] * q[3])
    w, x, y, z = (t * inv_q for t in q)
    rg = [
        [1.0 - 2.0 * (y * y + z * z), 2.0 * (x * y - w * z), 2.0 * (x * z + w * y)],
        [2.0 * (x * y + w * z), 1.0 - 2.0 * (x * x + z * z), 2.0 * (y * z - w * x)],
        [2.0 * (x * z - w * y), 2.0 * (y * z + w * x), 1.0 - 2.0 * (x * x + y * y)],
    ]
    scales = [jnp.exp(rows[3 + k]) for k in range(3)]
    sx = [jx * (rot[0][j] - xn * rot[2][j]) for j in range(3)]
    sy = [jy * (rot[1][j] - yn * rot[2][j]) for j in range(3)]
    bx = [(sx[0] * rg[0][k] + sx[1] * rg[1][k] + sx[2] * rg[2][k]) * scales[k] for k in range(3)]
    by = [(sy[0] * rg[0][k] + sy[1] * rg[1][k] + sy[2] * rg[2][k]) * scales[k] for k in range(3)]
    cxx = bx[0] * bx[0] + bx[1] * bx[1] + bx[2] * bx[2] + 0.3
    cxy = bx[0] * by[0] + bx[1] * by[1] + bx[2] * by[2]
    cyy = by[0] * by[0] + by[1] * by[1] + by[2] * by[2] + 0.3
    inv_det = 1.0 / (cxx * cyy - cxy * cxy)
    opacity = 1.0 / (1.0 + jnp.exp(-rows[10]))
    view = [m[j] + (rot[0][j] * shift[0] + rot[1][j] * shift[1] + rot[2][j] * shift[2]) for j in range(3)]
    inv_len = 1.0 / jnp.sqrt(view[0] * view[0] + view[1] * view[1] + view[2] * view[2])
    dx, dy, dz = (t * inv_len for t in view)
    xx, yy, zz = dx * dx, dy * dy, dz * dz
    basis = [
        -sh_one * dy,
        sh_one * dz,
        -sh_one * dx,
        sh_two[0] * dx * dy,
        sh_two[1] * dy * dz,
        sh_two[2] * (2.0 * zz - xx - yy),
        sh_two[3] * dx * dz,
        sh_two[4] * (xx - yy),
        sh_three[0] * dy * (3.0 * xx - yy),
        sh_three[1] * dx * dy * dz,
        sh_three[2] * dy * (4.0 * zz - xx - yy),
        sh_three[3] * dz * (2.0 * zz - 3.0 * xx - 3.0 * yy),
        sh_three[4] * dx * (4.0 * zz - xx - yy),
        sh_three[5] * dz * (xx - yy),
        sh_three[6] * dx * (xx - 3.0 * yy),
    ]
    colour = []
    for c in range(3):
        total = 0.5 + sh_zero * rows[11 + c]
        for k in range(1, 16):
            total = total + basis[k - 1] * rows[11 + 3 * k + c]
        colour.append(total)
    return [u, v, cyy * inv_det, -cxy * inv_det, cxx * inv_det, *colour, opacity]


def split(value, parts):
    out = []
    for _ in range(parts - 1):
        piece = value.astype(BF16)
        out.append(piece)
        value = value - piece.astype(F32)
    out.append(value.astype(BF16))
    return out


def dot_nn(a, b, precision=None):
    return lax.dot_general(a, b, (((1,), (0,)), ((), ())), precision=precision, preferred_element_type=F32)


def dot_nt(a, b, precision=None):
    return lax.dot_general(a, b, (((1,), (1,)), ((), ())), precision=precision, preferred_element_type=F32)


def where_equal(a, b):
    return jnp.where(a == b, 1.0, 0.0).astype(BF16)


def iota(shape, dim):
    return lax.broadcasted_iota(jnp.int32, shape, dim)


def place(x, z, c):
    return (x * 16 + z) * 2 + c


def as_message(feats):
    blocks = [feats[:, k * 128 : (k + 1) * 128] for k in range(4)]
    both = jnp.concatenate(blocks + blocks, axis=0).T
    return jnp.where(iota((64, 128), 1) < 64, both[0:64], both[64:128])


def as_columns(rows):
    both = jnp.concatenate([rows, rows], axis=0).T
    left = iota((16, 128), 1) < 64
    blocks = [jnp.where(left, both[16 * k : 16 * k + 16], both[64 + 16 * k : 80 + 16 * k]) for k in range(4)]
    return jnp.concatenate(blocks, axis=1)


def natural(column, received):
    k = column >> 7
    if received:
        x, c = (column >> 3) & 3, (column >> 5) & 1
        z = ((column >> 6) & 1) * 8 + (column & 7)
    else:
        x, c, z = (column >> 4) & 3, (column >> 6) & 1, column & 15
    return x * 128 + z * 8 + c * 4 + k


def column_of(row):
    return ((row & 3) << 7) | (((row >> 2) & 1) << 6) | (row >> 3)


def reorder(values, received):
    n = len(values)
    row = iota((16, ROWS), 0)
    pieces = jnp.zeros((16, ROWS), F32)
    for i, value in enumerate(values):
        pieces = jnp.where(row == 2 * i, (value >> 6).astype(F32), pieces)
        pieces = jnp.where(row == 2 * i + 1, (value & 63).astype(F32), pieces)
    order = where_equal(iota((ROWS, ROWS), 0), natural(iota((ROWS, ROWS), 1), received))
    pieces = dot_nn(pieces.astype(BF16), order)
    return [pieces[2 * i : 2 * i + 1] * 64.0 + pieces[2 * i + 1 : 2 * i + 2] for i in range(n)]


def kernel(
    params,
    cam_in,
    send_rows_in,
    tiles_in,
    lists_in,
    counts_in,
    targets_in,
    gq,
    rendered,
    cam,
    send_rows,
    tiles,
    lists,
    counts,
    targets,
    lsem,
    pv,
    tail,
    pq,
    info,
    p3,
    oh,
    high,
    low,
    gs,
    fs,
    msg,
    mid,
    comp,
    got,
    ohr,
    upper,
    lower,
    fe,
    al,
    lk,
    bf,
    ws,
    sw2,
    rs,
    ge,
    psem,
    isend,
    irecv,
    zsend,
    zrecv,
    xsend,
    xrecv,
    near_sem,
    view_sem,
):
    me, my = lax.axis_index("gauss"), lax.axis_index("img")
    mx, mz, mc = me // 32, (me // 2) % 16, me % 2
    far_first = [8, 7, 9, 6, 10, 5, 11, 4, 12, 3, 13, 2, 14, 1, 15]
    z_peers = [(mz + j) % 16 for j in far_first]
    z_near = z_peers[7:]
    x_peers = [((mx + x) % 4, (mc + c) % 2) for x in (2, 1, 3, 0) for c in (0, 1)]
    x_others = x_peers[:6] + x_peers[7:]
    y_peers = [(my + y) % 4 for y in (2, 1, 3)]

    def tell(semaphore, device):
        pl.semaphore_signal(semaphore, inc=1, device_id=device, device_id_type=MESH)

    barrier = pltpu.get_barrier_semaphore()
    for z in z_near[:2]:
        tell(barrier, {"gauss": place(mx, z, mc)})
    for x, c in x_others:
        tell(barrier, {"gauss": place(x, mz, c)})
    for z in z_near[2:]:
        tell(barrier, {"gauss": place(mx, z, mc)})
    for y in y_peers:
        tell(barrier, {"img": y})

    loads = [
        pltpu.make_async_copy(source, target, lsem.at[n])
        for n, (source, target) in enumerate(
            [(send_rows_in, send_rows), (cam_in, cam), (lists_in, lists)]
            + [(tiles_in, tiles), (counts_in, counts), (targets_in, targets)]
        )
    ]
    loads[0].start()
    for part in range(4):
        columns = pl.ds(part * QUARTER, QUARTER)
        pltpu.make_async_copy(params.at[:, columns], pv.at[:, columns], psem).start()
    for copy in loads[1:]:
        copy.start()
    loads[0].wait()

    (chosen,) = reorder([send_rows[...]], False)

    @pl.loop(0, 64)
    def _(j):
        start = pl.multiple_of(j * 64, 64)
        gauss = (iota((64, ROWS), 0) + start).astype(F32)
        oh[pl.ds(start, 64), :] = where_equal(gauss, chosen)

    tail[...] = jnp.zeros((8, G_DEV), F32)
    pltpu.make_async_copy(params, pv, psem).wait()
    for copy in loads[1:]:
        copy.wait()

    @pl.loop(0, 16)
    def _(j):
        here = pl.ds(pl.multiple_of(j * 256, 256), 256)
        tail[0:3, here] = pv[56:PARAMS, here]
        whole = jnp.concatenate([pv[0:56, here], tail[:, here]], axis=0)
        for n, piece in enumerate(split(whole, 3)):
            p3[64 * n : 64 * (n + 1), here] = piece

    picked = dot_nn(p3[...], oh[...])
    gs[...] = picked[0:64] + picked[64:128] + picked[128:192]
    feats = project_rows([gs[f : f + 1, :] for f in range(PARAMS)], [cam[0, k] for k in range(16)])
    fs[8:16, :] = jnp.zeros((8, ROWS), F32)
    for f in range(FEATS):
        fs[f : f + 1, :] = feats[f]

    pl.semaphore_wait(barrier, 18)
    for z in z_near:
        tell(near_sem, {"gauss": place(mx, z, mc)})
    for y in y_peers:
        tell(view_sem, {"img": y})

    left = iota((8, 128), 1) < 64
    mine = mc * 4 + mx

    def halves(first, second):
        return jnp.where(left, first, pltpu.roll(second, 64, 1)), jnp.where(left, pltpu.roll(first, 64, 1), second)

    def send_z(turn):
        for z in z_peers:
            pltpu.make_async_remote_copy(
                src_ref=msg.at[turn, :, z], dst_ref=mid.at[turn, :, mz], send_sem=zsend.at[turn], recv_sem=zrecv.at[turn],
                device_id={"gauss": place(mx, z, mc)}, device_id_type=MESH,
            ).start()
        mid[turn, :, mz] = msg[turn, :, mz]

    def wait_z(turn, sems):
        span = mid.at[turn, :, pl.ds(0, 15)]
        pltpu.make_async_copy(span, span, sems.at[turn]).wait()

    def send_x(turn, y, slot):
        for x, c in x_peers if y is not my else x_others:
            pltpu.make_async_remote_copy(
                src_ref=comp.at[turn, c * 4 + x], dst_ref=got.at[slot, mine], send_sem=xsend.at[turn],
                recv_sem=xrecv.at[slot], device_id={"gauss": place(x, mz, c), "img": y}, device_id_type=MESH,
            ).start()
        if y is my:
            got[slot, mine] = comp[turn, mine]

    def wait_x(slot, count):
        span = got.at[slot, pl.ds(0, count)]
        pltpu.make_async_copy(span, span, xrecv.at[slot]).wait()

    def prepare():
        named = jnp.concatenate([lists[0, 0:1, :], lists[0, 1:2, :]], axis=1)
        named = column_of(named)

        @pl.loop(0, 8)
        def _(j):
            start = pl.multiple_of(j * 64, 64)
            ohr[pl.ds(start, 64), :] = where_equal(iota((64, ROWS), 0) + start, named)

        earlier = jnp.where(iota((LIST, LIST), 0) < iota((LIST, LIST), 1), 1.0, 0.0).astype(BF16)
        later = jnp.where(iota((LIST, LIST), 0) > iota((LIST, LIST), 1), 1.0, 0.0).astype(BF16)
        for n in range(2):
            upper[LIST * n : LIST * (n + 1), :] = earlier
            lower[LIST * n : LIST * (n + 1), :] = later
        rs[...] = jnp.zeros((2, 16, 256), F32)
        ge[8:16, :] = jnp.zeros((8, ROWS), F32)

    packed = as_message(fs[...])
    for x in range(4):
        comp[0, x], comp[0, 4 + x] = halves(packed[16 * x : 16 * x + 8], packed[16 * x + 8 : 16 * x + 16])
    send_x(0, my, 4)
    for k in range(16):
        info[my, k : k + 1, :] = jnp.zeros((1, 128), F32) + cam[0, k]
    for k in range(4):
        info[my, 16 + k : 17 + k, :] = send_rows[:, k * 128 : (k + 1) * 128].astype(F32)
    info[my, 20:24, :] = jnp.zeros((4, 128), F32)
    for n, y in enumerate(y_peers):
        pltpu.make_async_remote_copy(
            src_ref=info.at[my], dst_ref=info.at[my], send_sem=isend.at[n], recv_sem=irecv.at[n],
            device_id={"img": y}, device_id_type=MESH,
        ).start()
    wait_x(4, 7)
    for x in range(4):
        low_z, high_z = halves(got[4, x], got[4, 4 + x])
        msg.reshape(128, 128)[16 * x : 16 * x + 8, :] = low_z
        msg.reshape(128, 128)[16 * x + 8 : 16 * x + 16, :] = high_z
    pl.semaphore_wait(near_sem, 8)
    send_z(0)
    prepare()
    wait_z(0, zrecv)
    received = as_columns(mid.reshape(128, 128)[0:64, :])

    listed = dot_nn(jnp.concatenate(split(received, 3), axis=0), ohr[...])
    fe[...] = listed[0:16] + listed[16:32] + listed[32:48]

    def entry(f, t):
        return fe[f : f + 1, t * LIST : (t + 1) * LIST]

    pixel = iota((16, LIST), 0).astype(F32)
    off_x, quad_x, cross, quad_y, origin_y, weight = [], [], [], [], [], []
    for t in range(2):
        tile = tiles[0, t]
        off_x.append(entry(0, t) - (pixel + ((tile & 15) * 16).astype(F32)))
        origin_y.append(entry(1, t) - ((tile >> 4) * 16).astype(F32))
        quad_x.append(-0.5 * entry(2, t) * off_x[t] * off_x[t])
        cross.append(-entry(3, t))
        quad_y.append(-0.5 * entry(4, t))
        weight.append(jnp.where(iota((1, LIST), 1) < counts[0, t], entry(8, t), 0.0))

    def pixels(t, j):
        return pl.ds(pl.multiple_of(t * 256 + j * 16, 16), 16)

    @pl.loop(0, 16, unroll=16)
    def _(j):
        for t in range(2):
            here = pixels(t, j)
            off_y = origin_y[t] - lax.convert_element_type(j, F32)
            power = quad_x[t] + off_x[t] * (cross[t] * off_y) + quad_y[t] * off_y * off_y
            alpha = weight[t] * jnp.exp(power)
            al[here, :] = alpha
            for n, piece in enumerate(split(jnp.log(1.0 - alpha), 2)):
                lk[here, LIST * n : LIST * (n + 1)] = piece

    bf[...] = dot_nn(lk[...], upper[...])

    @pl.loop(0, 16, unroll=16)
    def _(j):
        for t in range(2):
            here = pixels(t, j)
            ws[here, :] = al[here, :] * jnp.exp(bf[here, :])

    grad_colour = []
    for t in range(2):
        shown = split(ws[t * 256 : (t + 1) * 256, :], 3)
        tints = split(fe[:, t * LIST : (t + 1) * LIST], 3)
        stacked = jnp.concatenate(tints, axis=0)
        colours = dot_nt(stacked, shown[0]) + dot_nt(stacked, shown[1]) + dot_nt(stacked, shown[2])
        colours = (colours[0:16] + colours[16:32] + colours[32:48])[5:8]
        rendered[0, :, t, :] = colours
        rs[t, 5:8, :] = colours - targets[0, :, t, :]
        resid = split(rs[t], 2)
        stacked = jnp.concatenate(resid, axis=0)
        tinted = dot_nn(stacked, shown[0]) + dot_nn(stacked, shown[1])
        grad_colour.append(tinted[5:8] + tinted[21:24])
        resid = [piece.astype(F32) for piece in resid]
        turned = jnp.concatenate([resid[0], resid[1], resid[0]], axis=0).T.astype(BF16)
        bf[t * 256 : (t + 1) * 256, :] = dot_nn(turned, jnp.concatenate([tints[0], tints[0], tints[1]], axis=0))

    @pl.loop(0, 16, unroll=16)
    def _(j):
        for t in range(2):
            here = pixels(t, j)
            share = bf[here, :] * ws[here, :]
            ws[here, :] = share
            for n, piece in enumerate(split(share, 2)):
                sw2[here, LIST * n : LIST * (n + 1)] = piece

    bf[...] = dot_nn(sw2[...], lower[...])

    for t in range(2):

        def moments(j, carry):
            here = pixels(t, j)
            alpha = al[here, :]
            off_y = origin_y[t] - lax.convert_element_type(j, F32)
            flow = ws[here, :] - bf[here, :] * (alpha / (1.0 - alpha))
            flow_y = flow * off_y
            return carry[0] + flow, carry[1] + flow_y, carry[2] + flow_y * off_y

        zero = jnp.zeros((16, LIST), F32)
        flow, flow_y, flow_yy = lax.fori_loop(0, 16, moments, (zero, zero, zero), unroll=16)

        def over(value):
            return jnp.sum(value, axis=0, keepdims=True)

        m_x, m_y = over(flow * off_x[t]), over(flow_y)
        a, b, c = entry(2, t), entry(3, t), entry(4, t)
        out = [
            -(a * m_x + b * m_y),
            -(b * m_x + c * m_y),
            -0.5 * over(flow * off_x[t] * off_x[t]),
            -over(flow_y * off_x[t]),
            -0.5 * over(flow_yy),
            grad_colour[t][0:1],
            grad_colour[t][1:2],
            grad_colour[t][2:3],
            over(flow) / entry(8, t),
        ]
        for f in range(FEATS):
            ge[f : f + 1, t * LIST : (t + 1) * LIST] = out[f]

    back = dot_nt(jnp.concatenate(split(ge[...], 2), axis=0), ohr[...])
    msg.reshape(128, 128)[64:128, :] = as_message(back[0:16] + back[16:32])
    pulls = []

    def look_ahead():
        for n in range(3):
            pltpu.make_async_copy(info.at[0], info.at[0], irecv.at[n]).wait()
            pltpu.make_async_copy(info.at[0], info.at[0], isend.at[n]).wait()
        rows = [
            jnp.concatenate([info[view, 16 + k : 17 + k, :] for k in range(4)], axis=1).astype(jnp.int32)
            for view in range(4)
        ]
        for view, picks in enumerate(reorder(rows, True)):
            place_in = (picks - (my * QUARTER).astype(F32)).astype(jnp.int32)
            high[view] = jnp.where(iota((8, ROWS), 0) == (place_in >> 7), 1.0, 0.0)
            low[view] = where_equal(iota((128, ROWS), 0), place_in & 127)
        for block in range(8):
            pq[block] = pv[:, pl.ds(pl.multiple_of(my * QUARTER + block * 128, 128), 128)]
        own = [pq[:, f, :] for f in range(PARAMS)]
        for view in [my] + y_peers:
            camera = [jnp.broadcast_to(info[view, k : k + 1, :], (8, 128)) for k in range(16)]
            pulls.append(jax.vjp(lambda rows, camera=camera: project_rows(rows, camera), own)[1])

    send_z(1)
    look_ahead()
    wait_z(1, zrecv)
    for x in range(4):
        whole = mid.reshape(128, 128)[64 + 16 * x : 80 + 16 * x, :]
        comp[1, x], comp[1, 4 + x] = halves(whole[0:8], whole[8:16])
    pl.semaphore_wait(view_sem, 3)
    for y in y_peers + [my]:
        send_x(1, y, my)
    for turn in range(2):
        wait_z(turn, zsend)

    def pulled(view, number, count):
        wait_x(view, count)
        cols = as_columns(got[view].reshape(64, 128))
        parts = [high[view] * cols[f : f + 1] for f in range(FEATS)] + [jnp.zeros((8, ROWS), F32)]
        parts = split(jnp.concatenate(parts, axis=0), 2)
        sums = dot_nt(jnp.concatenate(parts, axis=0), low[view])
        sums = sums[0:80] + sums[80:160]
        (out,) = pulls[number]([sums[8 * f : 8 * f + 8] for f in range(FEATS)])
        return out

    total = pulled(my, 0, 7)
    for n, y in enumerate(y_peers):
        total = [a + b for a, b in zip(total, pulled(y, n + 1, 8))]
    for f in range(PARAMS):
        gq[:, f, :] = total[f]
    span = comp.at[0, pl.ds(0, 7)]
    pltpu.make_async_copy(span, span, xsend.at[0]).wait()
    span = got.at[0, pl.ds(0, 7)]
    pltpu.make_async_copy(span, span, xsend.at[1]).wait()
    span = got.at[pl.ds(0, 3)]
    pltpu.make_async_copy(span, span, xsend.at[1]).wait()


def finish(blocks, shown, grads, rendered, block, small, into, out):
    reads = [pltpu.make_async_copy(blocks.at[b], block.at[b], into.at[b]) for b in range(8)]
    reads.append(pltpu.make_async_copy(shown, small, into.at[8]))
    for copy in reads:
        copy.start()
    writes = [pltpu.make_async_copy(block.at[b], grads.at[:, pl.ds(b * 128, 128)], out.at[b]) for b in range(8)]
    writes.append(pltpu.make_async_copy(small, rendered, out.at[8]))
    for read, write in zip(reads, writes):
        read.wait()
        write.start()
    for write in writes:
        write.wait()


def local(params, cameras, send_rows, tile_ids, lists, counts, targets):
    vmem, anywhere = (pl.BlockSpec(memory_space=s) for s in (pltpu.VMEM, pl.ANY))
    dma = pltpu.SemaphoreType.DMA
    blocks, shown = pl.pallas_call(
        kernel,
        out_shape=(
            jax.ShapeDtypeStruct((8, PARAMS, 128), F32),
            jax.ShapeDtypeStruct((1, 3, 2, 256), F32),
        ),
        in_specs=[anywhere] * 7,
        out_specs=(vmem, vmem),
        scratch_shapes=[
            pltpu.SMEM((1, 16), F32),
            pltpu.VMEM((1, ROWS), jnp.int32),
            pltpu.SMEM((1, 2), jnp.int32),
            pltpu.VMEM((1, 2, LIST), jnp.int32),
            pltpu.SMEM((1, 2), jnp.int32),
            pltpu.VMEM((1, 3, 2, 256), F32),
            dma((6,)),
            pltpu.VMEM((PARAMS, G_DEV), F32),
            pltpu.VMEM((8, G_DEV), F32),
            pltpu.VMEM((8, PARAMS, 128), F32),
            pltpu.VMEM((4, 24, 128), F32),
            pltpu.VMEM((192, G_DEV), BF16),
            pltpu.VMEM((G_DEV, ROWS), BF16),
            pltpu.VMEM((4, 8, ROWS), F32),
            pltpu.VMEM((4, 128, ROWS), BF16),
            pltpu.VMEM((64, ROWS), F32),
            pltpu.VMEM((16, ROWS), F32),
            pltpu.VMEM((2, 4, 16, 1, 128), F32),
            pltpu.VMEM((2, 4, 16, 1, 128), F32),
            pltpu.VMEM((2, 8, 8, 128), F32),
            pltpu.VMEM((5, 8, 8, 128), F32),
            pltpu.VMEM((ROWS, ROWS), BF16),
            pltpu.VMEM((2 * LIST, LIST), BF16),
            pltpu.VMEM((2 * LIST, LIST), BF16),
            pltpu.VMEM((16, ROWS), F32),
            pltpu.VMEM((512, LIST), F32),
            pltpu.VMEM((512, 2 * LIST), BF16),
            pltpu.VMEM((512, LIST), F32),
            pltpu.VMEM((512, LIST), F32),
            pltpu.VMEM((512, 2 * LIST), BF16),
            pltpu.VMEM((2, 16, 256), F32),
            pltpu.VMEM((16, ROWS), F32),
            dma,
            dma((3,)),
            dma((3,)),
            dma((2,)),
            dma((2,)),
            dma((2,)),
            dma((5,)),
            pltpu.SemaphoreType.REGULAR,
            pltpu.SemaphoreType.REGULAR,
        ],
        compiler_params=pltpu.CompilerParams(
            collective_id=0, has_side_effects=True, vmem_limit_bytes=60 * 1024 * 1024
        ),
    )(params, cameras, send_rows, tile_ids, lists, counts, jnp.transpose(targets, (0, 2, 1, 3)))
    grads, shown = pl.pallas_call(
        finish,
        out_shape=(
            jax.ShapeDtypeStruct((PARAMS, QUARTER), F32),
            jax.ShapeDtypeStruct((1, 3, 2, 256), F32),
        ),
        in_specs=[anywhere, anywhere],
        out_specs=(anywhere, anywhere),
        scratch_shapes=[
            pltpu.VMEM((8, PARAMS, 128), F32),
            pltpu.VMEM((1, 3, 2, 256), F32),
            dma((9,)),
            dma((9,)),
        ],
        compiler_params=pltpu.CompilerParams(vmem_limit_bytes=60 * 1024 * 1024),
    )(blocks, shown)
    return grads, jnp.transpose(shown, (0, 2, 1, 3))


def solution(mesh):
    placed = (
        P(None, "gauss"),
        P("img", None),
        P("img", "gauss"),
        P("img", "gauss"),
        P("img", "gauss", None),
        P("img", "gauss"),
        P("img", "gauss", None, None),
    )
    return jax.shard_map(
        local,
        mesh=mesh,
        in_specs=placed,
        out_specs=(P(None, ("gauss", "img")), P("img", "gauss", None, None)),
        check_vma=False,
    )
```

time: 56.4 us -> 44.2 us (0.78)
  Pallas kernels: 52.2 us -> 43.3 us
  local copies, waits for them, and re-layouts: 3.26 us -> 0 us
    pallas_call x1 -> x2, Pallas kernels: 52.2 us -> 43.3 us  [the longest x1 41.7 us: local(): pl.pallas_call(kernel, out_shape=(jax.ShapeDtypeStruct((8, PARAMS, 128),...]
    unnamed x14 -> x0, local copies, waits for them, and re-layouts: 2.67 us -> none
    pallas_call x1 -> x0, local copies, waits for them, and re-layouts: 0.6 us -> none  [local(): pl.pallas_call(kernel, out_shape=(jax.ShapeDtypeStruct((PARAMS, QUARTER),...]
where the time goes in v2:
time: 44.2 us; the launch traced here: 43.9 us
  Pallas kernels  43.3 us (98%)
  between operations  0.64 us (1%)
    pallas_call x1, Pallas kernels, local(): pl.pallas_call(kernel, out_shape=(jax.ShapeDtypeStruct((8, PARAMS, 128),...  41.7 us
    pallas_call x1, Pallas kernels, local(): pl.pallas_call(finish, out_shape=(jax.ShapeDtypeStruct((PARAMS, QUARTER),...  1.63 us

profile of v2, /device:TPU:1, one launch (start us, length us, event | category | flops | bytes accessed | tf_op | source)
XLA Modules:
  0.0 43.9 jit_solution(12755807423947774318)
XLA Ops:
  0.6 41.7 %shard_map.86 = (f32[8,59,128]{2,1,0:T(8,128)}, f32[1,3,2,256]{3,2,1,0:T(2,128)}) custom-call(f32[59,4096]{1,0:T(8,128)} %params.1, f32[1,16]{1,0:T(1,128)} %cam_in.1, s32[1,512]{1,0:T(1,128)} %send_rows_in.1, s32[1,2]{1,0:T(1,128)} %tiles_in.1, s32[1,2,256]{2,1,0:T(2,128)} %lists_in.1, s32[1,2]{1,0:T(1,128)} %counts_in.1, f32[1,3,2,256]{3,2,1,0:T(2,128)} %bitcast.2), custom_call_target="tpu_custom_call" | custom-call | tf_op jit(solution)/shard_map/pallas_call | solution.py:532
  42.3 1.6 %shard_map.87 = (f32[59,1024]{1,0:T(8,128)}, f32[1,3,2,256]{3,2,1,0:T(2,128)}) custom-call(f32[8,59,128]{2,1,0:T(8,128)} %get-tuple-element.6.blocks, f32[1,3,2,256]{3,2,1,0:T(2,128)} %get-tuple-element.7.shown), custom_call_target="tpu_custom_call" | custom-call | tf_op jit(solution)/shard_map/pallas_call | solution.py:587

commit v3 on v2

--- a/solution.py
+++ b/solution.py
@@ -484,7 +484,7 @@
         whole = mid.reshape(128, 128)[64 + 16 * x : 80 + 16 * x, :]
         comp[1, x], comp[1, 4 + x] = halves(whole[0:8], whole[8:16])
     pl.semaphore_wait(view_sem, 3)
-    for y in y_peers + [my]:
+    for y in (y_peers[0], my, y_peers[1], y_peers[2]):
         send_x(1, y, my)
     for turn in range(2):
         wait_z(turn, zsend)
@@ -500,7 +500,7 @@
         return out
 
     total = pulled(my, 0, 7)
-    for n, y in enumerate(y_peers):
+    for n, y in ((1, y_peers[1]), (2, y_peers[2]), (0, y_peers[0])):
         total = [a + b for a, b in zip(total, pulled(y, n + 1, 8))]
     for f in range(PARAMS):
         gq[:, f, :] = total[f]
@@ -512,23 +512,19 @@
     pltpu.make_async_copy(span, span, xsend.at[1]).wait()
 
 
-def finish(blocks, shown, grads, rendered, block, small, into, out):
-    reads = [pltpu.make_async_copy(blocks.at[b], block.at[b], into.at[b]) for b in range(8)]
-    reads.append(pltpu.make_async_copy(shown, small, into.at[8]))
-    for copy in reads:
+def finish(blocks, shown, grads, rendered, sem):
+    copies = [pltpu.make_async_copy(blocks.at[b], grads.at[:, pl.ds(b * 128, 128)], sem.at[b]) for b in range(8)]
+    copies.append(pltpu.make_async_copy(shown, rendered, sem.at[8]))
+    for copy in copies:
         copy.start()
-    writes = [pltpu.make_async_copy(block.at[b], grads.at[:, pl.ds(b * 128, 128)], out.at[b]) for b in range(8)]
-    writes.append(pltpu.make_async_copy(small, rendered, out.at[8]))
-    for read, write in zip(reads, writes):
-        read.wait()
-        write.start()
-    for write in writes:
-        write.wait()
+    for copy in copies:
+        copy.wait()
 
 
 def local(params, cameras, send_rows, tile_ids, lists, counts, targets):
     vmem, anywhere = (pl.BlockSpec(memory_space=s) for s in (pltpu.VMEM, pl.ANY))
     dma = pltpu.SemaphoreType.DMA
+    operands = (params, cameras, send_rows, tile_ids, lists, counts, jnp.transpose(targets, (0, 2, 1, 3)))
     blocks, shown = pl.pallas_call(
         kernel,
         out_shape=(
@@ -581,9 +577,9 @@
             pltpu.SemaphoreType.REGULAR,
         ],
         compiler_params=pltpu.CompilerParams(
-            collective_id=0, has_side_effects=True, vmem_limit_bytes=60 * 1024 * 1024
+            collective_id=0, has_side_effects=True, vmem_limit_bytes=32 * 1024 * 1024
         ),
-    )(params, cameras, send_rows, tile_ids, lists, counts, jnp.transpose(targets, (0, 2, 1, 3)))
+    )(*(pltpu.with_memory_space_constraint(operand, pltpu.HBM) for operand in operands))
     grads, shown = pl.pallas_call(
         finish,
         out_shape=(
@@ -592,14 +588,8 @@
         ),
         in_specs=[anywhere, anywhere],
         out_specs=(anywhere, anywhere),
-        scratch_shapes=[
-            pltpu.VMEM((8, PARAMS, 128), F32),
-            pltpu.VMEM((1, 3, 2, 256), F32),
-            dma((9,)),
-            dma((9,)),
-        ],
-        compiler_params=pltpu.CompilerParams(vmem_limit_bytes=60 * 1024 * 1024),
-    )(blocks, shown)
+        scratch_shapes=[dma((9,))],
+    )(*(pltpu.with_memory_space_constraint(part, pltpu.VMEM) for part in (blocks, shown)))
     return grads, jnp.transpose(shown, (0, 2, 1, 3))
 
 

time: 44.2 us -> 42.4 us (0.959)
  Pallas kernels: 43.3 us -> 41.7 us
    pallas_call x1, Pallas kernels: 1.63 us -> 0.78 us  [local(): pl.pallas_call(finish, out_shape=(jax.ShapeDtypeStruct((PARAMS, QUARTER),...]
    pallas_call x1, Pallas kernels: 41.7 us -> 40.9 us  [local(): pl.pallas_call(kernel, out_shape=(jax.ShapeDtypeStruct((8, PARAMS, 128),...]
where the time goes in v3:
time: 42.4 us; the launch traced here: 42.3 us
  Pallas kernels  41.7 us (98%)
  between operations  0.64 us (2%)
    pallas_call x1, Pallas kernels, local(): pl.pallas_call(kernel, out_shape=(jax.ShapeDtypeStruct((8, PARAMS, 128),...  40.9 us

profile of v3, /device:TPU:1, one launch (start us, length us, event | category | flops | bytes accessed | tf_op | source)
XLA Modules:
  0.0 42.3 jit_solution(12983491347017845303)
XLA Ops:
  0.6 40.9 %shard_map.86 = (f32[8,59,128]{2,1,0:T(8,128)S(1)}, f32[1,3,2,256]{3,2,1,0:T(2,128)S(1)}) custom-call(f32[59,4096]{1,0:T(8,128)} %params.1, f32[1,16]{1,0:T(1,128)} %cam_in.1, s32[1,512]{1,0:T(1,128)} %send_rows_in.1, s32[1,2]{1,0:T(1,128)} %tiles_in.1, s32[1,2,256]{2,1,0:T(2,128)} %lists_in.1, s32[1,2]{1,0:T(1,128)} %counts_in.1, f32[1,3,2,256]{3,2,1,0:T(2,128)} %bitcast.2), custom_call_target="tpu_custom_call" | custom-call | tf_op jit(solution)/shard_map/pallas_call | solution.py:528
  41.5 0.8 %shard_map.87 = (f32[59,1024]{1,0:T(8,128)}, f32[1,3,2,256]{3,2,1,0:T(2,128)}) custom-call(f32[8,59,128]{2,1,0:T(8,128)S(1)} %get-tuple-element.6.blocks, f32[1,3,2,256]{3,2,1,0:T(2,128)S(1)} %get-tuple-element.7.shown), custom_call_target="tpu_custom_call" | custom-call | tf_op jit(solution)/shard_map/pallas_call | solution.py:583

commit v4 on v3

--- a/solution.py
+++ b/solution.py
@@ -191,6 +191,8 @@
     comp,
     got,
     ohr,
+    ohs,
+    names,
     upper,
     lower,
     fe,
@@ -277,7 +279,7 @@
         fs[f : f + 1, :] = feats[f]
 
     pl.semaphore_wait(barrier, 18)
-    for z in z_near:
+    for z in z_near[:2]:
         tell(near_sem, {"gauss": place(mx, z, mc)})
     for y in y_peers:
         tell(view_sem, {"img": y})
@@ -300,14 +302,11 @@
         span = mid.at[turn, :, pl.ds(0, 15)]
         pltpu.make_async_copy(span, span, sems.at[turn]).wait()
 
-    def send_x(turn, y, slot):
-        for x, c in x_peers if y is not my else x_others:
-            pltpu.make_async_remote_copy(
-                src_ref=comp.at[turn, c * 4 + x], dst_ref=got.at[slot, mine], send_sem=xsend.at[turn],
-                recv_sem=xrecv.at[slot], device_id={"gauss": place(x, mz, c), "img": y}, device_id_type=MESH,
-            ).start()
-        if y is my:
-            got[slot, mine] = comp[turn, mine]
+    def send_x(turn, x, c, y, slot):
+        pltpu.make_async_remote_copy(
+            src_ref=comp.at[turn, c * 4 + x], dst_ref=got.at[slot, mine], send_sem=xsend.at[turn],
+            recv_sem=xrecv.at[slot], device_id={"gauss": place(x, mz, c), "img": y}, device_id_type=MESH,
+        ).start()
 
     def wait_x(slot, count):
         span = got.at[slot, pl.ds(0, count)]
@@ -316,11 +315,13 @@
     def prepare():
         named = jnp.concatenate([lists[0, 0:1, :], lists[0, 1:2, :]], axis=1)
         named = column_of(named)
+        names[...] = jnp.broadcast_to(named.astype(F32), (8, ROWS)).T
 
         @pl.loop(0, 8)
         def _(j):
             start = pl.multiple_of(j * 64, 64)
             ohr[pl.ds(start, 64), :] = where_equal(iota((64, ROWS), 0) + start, named)
+            ohs[pl.ds(start, 64), :] = where_equal(iota((64, ROWS), 1).astype(F32), names[pl.ds(start, 64), 0:1])
 
         earlier = jnp.where(iota((LIST, LIST), 0) < iota((LIST, LIST), 1), 1.0, 0.0).astype(BF16)
         later = jnp.where(iota((LIST, LIST), 0) > iota((LIST, LIST), 1), 1.0, 0.0).astype(BF16)
@@ -333,7 +334,9 @@
     packed = as_message(fs[...])
     for x in range(4):
         comp[0, x], comp[0, 4 + x] = halves(packed[16 * x : 16 * x + 8], packed[16 * x + 8 : 16 * x + 16])
-    send_x(0, my, 4)
+    for x, c in x_others:
+        send_x(0, x, c, my, 4)
+    got[4, mine] = comp[0, mine]
     for k in range(16):
         info[my, k : k + 1, :] = jnp.zeros((1, 128), F32) + cam[0, k]
     for k in range(4):
@@ -349,7 +352,7 @@
         low_z, high_z = halves(got[4, x], got[4, 4 + x])
         msg.reshape(128, 128)[16 * x : 16 * x + 8, :] = low_z
         msg.reshape(128, 128)[16 * x + 8 : 16 * x + 16, :] = high_z
-    pl.semaphore_wait(near_sem, 8)
+    pl.semaphore_wait(near_sem, 2)
     send_z(0)
     prepare()
     wait_z(0, zrecv)
@@ -454,7 +457,7 @@
         for f in range(FEATS):
             ge[f : f + 1, t * LIST : (t + 1) * LIST] = out[f]
 
-    back = dot_nt(jnp.concatenate(split(ge[...], 2), axis=0), ohr[...])
+    back = dot_nn(jnp.concatenate(split(ge[...], 2), axis=0), ohs[...])
     msg.reshape(128, 128)[64:128, :] = as_message(back[0:16] + back[16:32])
     pulls = []
 
@@ -469,7 +472,7 @@
         for view, picks in enumerate(reorder(rows, True)):
             place_in = (picks - (my * QUARTER).astype(F32)).astype(jnp.int32)
             high[view] = jnp.where(iota((8, ROWS), 0) == (place_in >> 7), 1.0, 0.0)
-            low[view] = where_equal(iota((128, ROWS), 0), place_in & 127)
+            low[view] = jnp.where(iota((128, ROWS), 0) == (place_in & 127), 1.0, 0.0).T.astype(BF16)
         for block in range(8):
             pq[block] = pv[:, pl.ds(pl.multiple_of(my * QUARTER + block * 128, 128), 128)]
         own = [pq[:, f, :] for f in range(PARAMS)]
@@ -484,24 +487,29 @@
         whole = mid.reshape(128, 128)[64 + 16 * x : 80 + 16 * x, :]
         comp[1, x], comp[1, 4 + x] = halves(whole[0:8], whole[8:16])
     pl.semaphore_wait(view_sem, 3)
-    for y in (y_peers[0], my, y_peers[1], y_peers[2]):
-        send_x(1, y, my)
+    steps = [(x, c, y) for x in range(4) for c in range(2) for y in range(4) if (x, c, y) != (0, 0, 0)]
+    steps.sort(key=lambda step: -min(step[0], 4 - step[0]) - min(step[2], 4 - step[2]))
+    for x, c, y in steps:
+        send_x(1, (mx + x) % 4, (mc + c) % 2, (my + y) % 4, my)
+    got[my, mine] = comp[1, mine]
     for turn in range(2):
         wait_z(turn, zsend)
 
-    def pulled(view, number, count):
-        wait_x(view, count)
+    def pulled(view, number):
         cols = as_columns(got[view].reshape(64, 128))
         parts = [high[view] * cols[f : f + 1] for f in range(FEATS)] + [jnp.zeros((8, ROWS), F32)]
         parts = split(jnp.concatenate(parts, axis=0), 2)
-        sums = dot_nt(jnp.concatenate(parts, axis=0), low[view])
+        sums = dot_nn(jnp.concatenate(parts, axis=0), low[view])
         sums = sums[0:80] + sums[80:160]
         (out,) = pulls[number]([sums[8 * f : 8 * f + 8] for f in range(FEATS)])
         return out
 
-    total = pulled(my, 0, 7)
+    wait_x(my, 7)
+    total = pulled(my, 0)
+    for y in y_peers:
+        wait_x(y, 8)
     for n, y in ((1, y_peers[1]), (2, y_peers[2]), (0, y_peers[0])):
-        total = [a + b for a, b in zip(total, pulled(y, n + 1, 8))]
+        total = [a + b for a, b in zip(total, pulled(y, n + 1))]
     for f in range(PARAMS):
         gq[:, f, :] = total[f]
     span = comp.at[0, pl.ds(0, 7)]
@@ -528,8 +536,8 @@
     blocks, shown = pl.pallas_call(
         kernel,
         out_shape=(
-            jax.ShapeDtypeStruct((8, PARAMS, 128), F32),
-            jax.ShapeDtypeStruct((1, 3, 2, 256), F32),
+            pltpu.VMEM((8, PARAMS, 128), F32),
+            pltpu.VMEM((1, 3, 2, 256), F32),
         ),
         in_specs=[anywhere] * 7,
         out_specs=(vmem, vmem),
@@ -548,7 +556,7 @@
             pltpu.VMEM((192, G_DEV), BF16),
             pltpu.VMEM((G_DEV, ROWS), BF16),
             pltpu.VMEM((4, 8, ROWS), F32),
-            pltpu.VMEM((4, 128, ROWS), BF16),
+            pltpu.VMEM((4, ROWS, 128), BF16),
             pltpu.VMEM((64, ROWS), F32),
             pltpu.VMEM((16, ROWS), F32),
             pltpu.VMEM((2, 4, 16, 1, 128), F32),
@@ -556,6 +564,8 @@
             pltpu.VMEM((2, 8, 8, 128), F32),
             pltpu.VMEM((5, 8, 8, 128), F32),
             pltpu.VMEM((ROWS, ROWS), BF16),
+            pltpu.VMEM((ROWS, ROWS), BF16),
+            pltpu.VMEM((ROWS, 8), F32),
             pltpu.VMEM((2 * LIST, LIST), BF16),
             pltpu.VMEM((2 * LIST, LIST), BF16),
             pltpu.VMEM((16, ROWS), F32),

time: 42.4 us -> 41.9 us (0.988)
  Pallas kernels: 41.7 us -> 41.2 us
    pallas_call x1, Pallas kernels: 40.9 us -> 40.4 us  [local(): pl.pallas_call(kernel, out_shape=(pltpu.VMEM((8, PARAMS, 128), F32), pltp...]
where the time goes in v4:
time: 41.9 us; the launch traced here: 41.8 us
  Pallas kernels  41.2 us (98%)
  between operations  0.64 us (2%)
    pallas_call x1, Pallas kernels, local(): pl.pallas_call(kernel, out_shape=(pltpu.VMEM((8, PARAMS, 128), F32), pltp...  40.4 us

profile of v4, /device:TPU:1, one launch (start us, length us, event | category | flops | bytes accessed | tf_op | source)
XLA Modules:
  0.0 41.8 jit_solution(14849281012107336516)
XLA Ops:
  0.6 40.4 %shard_map.86 = (f32[8,59,128]{2,1,0:T(8,128)S(1)}, f32[1,3,2,256]{3,2,1,0:T(2,128)S(1)}) custom-call(f32[59,4096]{1,0:T(8,128)} %params.1, f32[1,16]{1,0:T(1,128)} %cam_in.1, s32[1,512]{1,0:T(1,128)} %send_rows_in.1, s32[1,2]{1,0:T(1,128)} %tiles_in.1, s32[1,2,256]{2,1,0:T(2,128)} %lists_in.1, s32[1,2]{1,0:T(1,128)} %counts_in.1, f32[1,3,2,256]{3,2,1,0:T(2,128)} %bitcast.2), custom_call_target="tpu_custom_call" | custom-call | tf_op jit(solution)/shard_map/pallas_call | solution.py:536
  41.0 0.8 %shard_map.87 = (f32[59,1024]{1,0:T(8,128)}, f32[1,3,2,256]{3,2,1,0:T(2,128)}) custom-call(f32[8,59,128]{2,1,0:T(8,128)S(1)} %get-tuple-element.6.blocks, f32[1,3,2,256]{3,2,1,0:T(2,128)S(1)} %get-tuple-element.7.shown), custom_call_target="tpu_custom_call" | custom-call | tf_op jit(solution)/shard_map/pallas_call | solution.py:593

commit v5 on v4

--- a/solution.py
+++ b/solution.py
@@ -277,18 +277,20 @@
     fs[8:16, :] = jnp.zeros((8, ROWS), F32)
     for f in range(FEATS):
         fs[f : f + 1, :] = feats[f]
+    left = iota((8, 128), 1) < 64
+    mine = mc * 4 + mx
+
+    def halves(first, second):
+        return jnp.where(left, first, pltpu.roll(second, 64, 1)), jnp.where(left, pltpu.roll(first, 64, 1), second)
+
+    packed = as_message(fs[...])
+    for x in range(4):
+        comp[0, x], comp[0, 4 + x] = halves(packed[16 * x : 16 * x + 8], packed[16 * x + 8 : 16 * x + 16])
+    got[4, mine] = comp[0, mine]
 
     pl.semaphore_wait(barrier, 18)
     for z in z_near[:2]:
         tell(near_sem, {"gauss": place(mx, z, mc)})
-    for y in y_peers:
-        tell(view_sem, {"img": y})
-
-    left = iota((8, 128), 1) < 64
-    mine = mc * 4 + mx
-
-    def halves(first, second):
-        return jnp.where(left, first, pltpu.roll(second, 64, 1)), jnp.where(left, pltpu.roll(first, 64, 1), second)
 
     def send_z(turn):
         for z in z_peers:
@@ -331,22 +333,15 @@
         rs[...] = jnp.zeros((2, 16, 256), F32)
         ge[8:16, :] = jnp.zeros((8, ROWS), F32)
 
-    packed = as_message(fs[...])
-    for x in range(4):
-        comp[0, x], comp[0, 4 + x] = halves(packed[16 * x : 16 * x + 8], packed[16 * x + 8 : 16 * x + 16])
     for x, c in x_others:
         send_x(0, x, c, my, 4)
-    got[4, mine] = comp[0, mine]
+    for y in y_peers:
+        tell(view_sem, {"img": y})
     for k in range(16):
         info[my, k : k + 1, :] = jnp.zeros((1, 128), F32) + cam[0, k]
     for k in range(4):
         info[my, 16 + k : 17 + k, :] = send_rows[:, k * 128 : (k + 1) * 128].astype(F32)
     info[my, 20:24, :] = jnp.zeros((4, 128), F32)
-    for n, y in enumerate(y_peers):
-        pltpu.make_async_remote_copy(
-            src_ref=info.at[my], dst_ref=info.at[my], send_sem=isend.at[n], recv_sem=irecv.at[n],
-            device_id={"img": y}, device_id_type=MESH,
-        ).start()
     wait_x(4, 7)
     for x in range(4):
         low_z, high_z = halves(got[4, x], got[4, 4 + x])
@@ -354,6 +349,11 @@
         msg.reshape(128, 128)[16 * x + 8 : 16 * x + 16, :] = high_z
     pl.semaphore_wait(near_sem, 2)
     send_z(0)
+    for n, y in enumerate(y_peers):
+        pltpu.make_async_remote_copy(
+            src_ref=info.at[my], dst_ref=info.at[my], send_sem=isend.at[n], recv_sem=irecv.at[n],
+            device_id={"img": y}, device_id_type=MESH,
+        ).start()
     prepare()
     wait_z(0, zrecv)
     received = as_columns(mid.reshape(128, 128)[0:64, :])

time: 41.9 us -> 42.1 us (level)
  no operation moved by 1% of the time
where the time goes in v5:
time: 42.1 us; the launch traced here: 42 us
  Pallas kernels  41.3 us (98%)
  between operations  0.64 us (2%)
    pallas_call x1, Pallas kernels, local(): pl.pallas_call(kernel, out_shape=(pltpu.VMEM((8, PARAMS, 128), F32), pltp...  40.5 us

profile of v5, /device:TPU:1, one launch (start us, length us, event | category | flops | bytes accessed | tf_op | source)
XLA Modules:
  0.0 42.0 jit_solution(923731775990304629)
XLA Ops:
  0.6 40.5 %shard_map.86 = (f32[8,59,128]{2,1,0:T(8,128)S(1)}, f32[1,3,2,256]{3,2,1,0:T(2,128)S(1)}) custom-call(f32[59,4096]{1,0:T(8,128)} %params.1, f32[1,16]{1,0:T(1,128)} %cam_in.1, s32[1,512]{1,0:T(1,128)} %send_rows_in.1, s32[1,2]{1,0:T(1,128)} %tiles_in.1, s32[1,2,256]{2,1,0:T(2,128)} %lists_in.1, s32[1,2]{1,0:T(1,128)} %counts_in.1, f32[1,3,2,256]{3,2,1,0:T(2,128)} %bitcast.2), custom_call_target="tpu_custom_call" | custom-call | tf_op jit(solution)/shard_map/pallas_call | solution.py:536
  41.2 0.8 %shard_map.87 = (f32[59,1024]{1,0:T(8,128)}, f32[1,3,2,256]{3,2,1,0:T(2,128)}) custom-call(f32[8,59,128]{2,1,0:T(8,128)S(1)} %get-tuple-element.6.blocks, f32[1,3,2,256]{3,2,1,0:T(2,128)S(1)} %get-tuple-element.7.shown), custom_call_target="tpu_custom_call" | custom-call | tf_op jit(solution)/shard_map/pallas_call | solution.py:593

commit v6 on v4

--- a/solution.py
+++ b/solution.py
@@ -290,13 +290,12 @@
     def halves(first, second):
         return jnp.where(left, first, pltpu.roll(second, 64, 1)), jnp.where(left, pltpu.roll(first, 64, 1), second)
 
-    def send_z(turn):
-        for z in z_peers:
+    def send_z(turn, peers):
+        for z in peers:
             pltpu.make_async_remote_copy(
                 src_ref=msg.at[turn, :, z], dst_ref=mid.at[turn, :, mz], send_sem=zsend.at[turn], recv_sem=zrecv.at[turn],
                 device_id={"gauss": place(mx, z, mc)}, device_id_type=MESH,
             ).start()
-        mid[turn, :, mz] = msg[turn, :, mz]
 
     def wait_z(turn, sems):
         span = mid.at[turn, :, pl.ds(0, 15)]
@@ -352,8 +351,10 @@
         low_z, high_z = halves(got[4, x], got[4, 4 + x])
         msg.reshape(128, 128)[16 * x : 16 * x + 8, :] = low_z
         msg.reshape(128, 128)[16 * x + 8 : 16 * x + 16, :] = high_z
+    send_z(0, z_near)
     pl.semaphore_wait(near_sem, 2)
-    send_z(0)
+    send_z(0, z_peers[:7])
+    mid[0, :, mz] = msg[0, :, mz]
     prepare()
     wait_z(0, zrecv)
     received = as_columns(mid.reshape(128, 128)[0:64, :])
@@ -480,7 +481,8 @@
             camera = [jnp.broadcast_to(info[view, k : k + 1, :], (8, 128)) for k in range(16)]
             pulls.append(jax.vjp(lambda rows, camera=camera: project_rows(rows, camera), own)[1])
 
-    send_z(1)
+    send_z(1, z_peers)
+    mid[1, :, mz] = msg[1, :, mz]
     look_ahead()
     wait_z(1, zrecv)
     for x in range(4):

time: 41.9 us -> 41.9 us (level)
  no operation moved by 1% of the time
where the time goes in v6:
time: 41.9 us; the launch traced here: 41.8 us
  Pallas kernels  41.2 us (98%)
  between operations  0.64 us (2%)
    pallas_call x1, Pallas kernels, local(): pl.pallas_call(kernel, out_shape=(pltpu.VMEM((8, PARAMS, 128), F32), pltp...  40.4 us

profile of v6, /device:TPU:1, one launch (start us, length us, event | category | flops | bytes accessed | tf_op | source)
XLA Modules:
  0.0 41.8 jit_solution(13362774342076254150)
XLA Ops:
  0.6 40.4 %shard_map.86 = (f32[8,59,128]{2,1,0:T(8,128)S(1)}, f32[1,3,2,256]{3,2,1,0:T(2,128)S(1)}) custom-call(f32[59,4096]{1,0:T(8,128)} %params.1, f32[1,16]{1,0:T(1,128)} %cam_in.1, s32[1,512]{1,0:T(1,128)} %send_rows_in.1, s32[1,2]{1,0:T(1,128)} %tiles_in.1, s32[1,2,256]{2,1,0:T(2,128)} %lists_in.1, s32[1,2]{1,0:T(1,128)} %counts_in.1, f32[1,3,2,256]{3,2,1,0:T(2,128)} %bitcast.2), custom_call_target="tpu_custom_call" | custom-call | tf_op jit(solution)/shard_map/pallas_call | solution.py:538
  41.0 0.8 %shard_map.87 = (f32[59,1024]{1,0:T(8,128)}, f32[1,3,2,256]{3,2,1,0:T(2,128)}) custom-call(f32[8,59,128]{2,1,0:T(8,128)S(1)} %get-tuple-element.6.blocks, f32[1,3,2,256]{3,2,1,0:T(2,128)S(1)} %get-tuple-element.7.shown), custom_call_target="tpu_custom_call" | custom-call | tf_op jit(solution)/shard_map/pallas_call | solution.py:595
